TPU v7x, 128 devices: a whole 4x4x4 slice. The times are simulated.
128 devices in a mesh: dp: 8 (over x_lo, z), shard: 16 (over y, x_hi, core).
Axes of the slice: x: 4 (x_hi: 2, x_lo: 2; x = x_hi * 2 + x_lo), y: 4, z: 4, core: 2. Of those that a mesh axis runs over, the one named last changes fastest.
Arguments:
- states: bfloat16 [110592, 5120], P(('dp', 'shard')), may hold values from -6 to 6
- readout: bfloat16 [110592, 512], P(('dp', 'shard')), may hold values from -0.119628906 to 0.119628906
- logp_shift: bfloat16 [110592], P(('dp', 'shard')), may hold values from -0.59765625 to 0.59765625
- advantage: bfloat16 [110592], P(('dp', 'shard')), may hold values from -6 to 6
- response_mask: int32 [110592], P(('dp', 'shard')), may hold values 0 or 1
- rollout_len: int32 [128], P(('dp', 'shard')), may hold values from 144 to 864, as said below
- dest_slot: int32 [110592], P(('dp', 'shard')), may hold values from -1 to 4607, as said below
- weight: float32 [5120, 512], P('shard'), may hold values from -0.078125 to 0.078125
- moment1: float32 [5120, 512], P('shard'), may hold values from -0.0006 to 0.0006
- moment2: float32 [5120, 512], P('shard'), may hold values from 1e-09 to 1e-07
Outputs:
- weight_out: float32 [5120, 512], P('shard')
- moment1_out: float32 [5120, 512], P('shard')
- moment2_out: float32 [5120, 512], P('shard')
Inputs may be any that keep to these rules, and one draw needn't show every extreme that they name: `rollout_len`: in each group of devices with one shard index, one device holds 864 live rows and the others between 144 and 288. `dest_slot`: live rows name distinct (dp index, slot) pairs within a group of devices with one shard index; at most 864 // 8 rows of one device name one dp index, and in each group one device sends exactly that many to every dp index.
All inputs are finite; a program needn't handle non-finite values. No bound on the sum of `response_mask` on one device may be relied on, other than what follows from the above.
Results may differ from a plain program's by a relative error of at most 0.0045.
Values may be sent and summed in bfloat16 or wider, within the bound.
A program may use at most 128 MiB of HBM per device.

v0:
```python
import jax
import jax.numpy as jnp
from jax import lax
from jax.sharding import PartitionSpec as P

BAL = 576
UPDATES = 2
PRIOR_STEPS = 100
MB = 288


BETA_ONE = 0.9
BETA_TWO = 0.999
LEARN_RATE = 0.001
DECAY_RATE = 0.01
ADAM_EPS = 1e-08
CLIP_EPS = 0.2


def surrogate_coeff(log_ratio, adv_rows, weights, token_total):
    prob_ratio = jnp.exp(log_ratio)
    clipped = jnp.clip(prob_ratio, 1.0 - CLIP_EPS, 1.0 + CLIP_EPS)
    chosen = (prob_ratio * adv_rows <= clipped * adv_rows).astype(jnp.float32)
    return -(weights / token_total) * adv_rows * prob_ratio * chosen


def adam_step(master, moment_one, moment_two, gradient, step_num):
    moment_one = BETA_ONE * moment_one + (1.0 - BETA_ONE) * gradient
    moment_two = BETA_TWO * moment_two + (1.0 - BETA_TWO) * gradient * gradient
    first_hat = moment_one / (1.0 - BETA_ONE**step_num)
    second_hat = moment_two / (1.0 - BETA_TWO**step_num)
    master = master - LEARN_RATE * (
        first_hat / (jnp.sqrt(second_hat) + ADAM_EPS) + DECAY_RATE * master
    )
    return (master, moment_one, moment_two)


def fold_columns(inputs_now, shard_rows):
    return jnp.dot(inputs_now, shard_rows, preferred_element_type=jnp.float32)


def grad_columns(inputs_now, scaled):
    return lax.dot_general(
        inputs_now, scaled, (((0,), (0,)), ((), ())), preferred_element_type=jnp.float32
    )


def body(
    states,
    readout,
    logp_shift,
    advantage,
    response_mask,
    rollout_len,
    dest_slot,
    weight,
    moment1,
    moment2,
):
    rows_in = states.shape[0]
    width = states.shape[1]
    groups = lax.axis_size("dp")
    slots_cap = rows_in // groups
    row_index = jnp.arange(rows_in, dtype=jnp.int32)
    live_rows = (row_index < rollout_len[0]) & (dest_slot >= 0)
    slot_index = jnp.where(live_rows, dest_slot % BAL, BAL)
    batch_shift, batch_adv, batch_weight = ([], [], [])
    owner_idx = jnp.where(live_rows, dest_slot // BAL, 0)
    onehot_owner = (
        (owner_idx[:, None] == jnp.arange(groups, dtype=jnp.int32)[None, :]) & live_rows[:, None]
    ).astype(jnp.int32)
    within = jnp.sum((jnp.cumsum(onehot_owner, axis=0) - 1) * onehot_owner, axis=1)
    send_pos = jnp.where(live_rows, owner_idx * slots_cap + within, rows_in)
    labels = jnp.stack([slot_index, response_mask], axis=1)
    send_states = jnp.zeros_like(states).at[send_pos].set(states, mode="drop")
    send_read = jnp.zeros_like(readout).at[send_pos].set(readout, mode="drop")
    send_shift = jnp.zeros_like(logp_shift).at[send_pos].set(logp_shift, mode="drop")
    send_adv = jnp.zeros_like(advantage).at[send_pos].set(advantage, mode="drop")
    send_labels = jnp.full_like(labels, BAL).at[send_pos].set(labels, mode="drop")
    got_states, got_read, got_shift, got_adv, got_labels = (
        lax.all_to_all(send_states, "dp", split_axis=0, concat_axis=0, tiled=True),
        lax.all_to_all(send_read, "dp", split_axis=0, concat_axis=0, tiled=True),
        lax.all_to_all(send_shift, "dp", split_axis=0, concat_axis=0, tiled=True),
        lax.all_to_all(send_adv, "dp", split_axis=0, concat_axis=0, tiled=True),
        lax.all_to_all(send_labels, "dp", split_axis=0, concat_axis=0, tiled=True),
    )
    target_slot = got_labels[:, 0]
    work_states = jnp.zeros((BAL, width), jnp.bfloat16).at[target_slot].set(got_states, mode="drop")
    work_read = (
        jnp.zeros((BAL, readout.shape[1]), jnp.bfloat16).at[target_slot].set(got_read, mode="drop")
    )
    work_shift = (
        jnp.zeros((BAL,), jnp.float32)
        .at[target_slot]
        .set(got_shift.astype(jnp.float32), mode="drop")
    )
    work_adv = (
        jnp.zeros((BAL,), jnp.float32).at[target_slot].set(got_adv.astype(jnp.float32), mode="drop")
    )
    work_weight = (
        jnp.zeros((BAL,), jnp.float32)
        .at[target_slot]
        .set(got_labels[:, 1].astype(jnp.float32), mode="drop")
    )
    set_states = work_states.reshape(UPDATES, MB, width)
    set_read = work_read.reshape(UPDATES, MB, readout.shape[1])
    set_of = list(range(UPDATES))
    for update in range(UPDATES):
        batch_shift.append(work_shift[update * MB : (update + 1) * MB])
        batch_adv.append(work_adv[update * MB : (update + 1) * MB])
        batch_weight.append(work_weight[update * MB : (update + 1) * MB])
    local_counts = [jnp.sum(batch_weight[update]) for update in range(UPDATES)]
    master, moment_one, moment_two = (weight, moment1, moment2)
    for update in range(UPDATES):
        total = jnp.maximum(lax.psum(local_counts[update], ("dp", "shard")), 1.0)
        compute_weight = master.astype(jnp.bfloat16)
        inputs_now = set_states[set_of[update]]
        read_now = set_read[set_of[update]].astype(jnp.float32)
        projected = fold_columns(
            inputs_now, lax.all_gather(compute_weight, "shard", axis=0, tiled=True)
        )
        log_ratio = batch_shift[update] + jnp.sum(projected * read_now, axis=1)
        coefficient = surrogate_coeff(log_ratio, batch_adv[update], batch_weight[update], total)
        scaled = (coefficient[:, None] * read_now).astype(jnp.bfloat16)
        gradient = lax.psum_scatter(
            grad_columns(inputs_now, scaled), "shard", scatter_dimension=0, tiled=True
        )
        gradient = lax.psum(gradient, "dp")
        master, moment_one, moment_two = adam_step(
            master, moment_one, moment_two, gradient, PRIOR_STEPS + update + 1
        )
    return (master, moment_one, moment_two)


def solution(mesh):
    return jax.shard_map(
        body,
        mesh=mesh,
        in_specs=(
            P(("dp", "shard"), None),
            P(("dp", "shard"), None),
            P(("dp", "shard")),
            P(("dp", "shard")),
            P(("dp", "shard")),
            P(("dp", "shard")),
            P(("dp", "shard")),
            P("shard", None),
            P("shard", None),
            P("shard", None),
        ),
        out_specs=(P("shard", None), P("shard", None), P("shard", None)),
        check_vma=False,
    )
```

profile of v0, /device:TPU:0, one launch (start us, length us, event | category | flops | bytes accessed | tf_op | source)
XLA Modules:
  0.0 776.1 jit_solution(9019218977131952950)
XLA Ops:
  14.4 8.8 %scatter_custom_fusion.3 = bf16[864]{0:T(1024)(128)(2,1)S(1)} fusion(s32[864]{0:T(1024)S(1)} %compare_select_fusion.1, bf16[864]{0:T(1024)(128)(2,1)} %param.12, bf16[]{:T(256)} %constant.23.clone.1), kind=kCustom, calls=%fused_computation.88 | custom fusion | bytes 2240 | tf_op jit(solution)/shard_map/scatter | solution.py:77
  23.9 6.3 all-to-all-start.2
  30.9 8.8 %scatter_custom_fusion.7 = bf16[864]{0:T(1024)(128)(2,1)S(1)} fusion(s32[864]{0:T(1024)S(1)} %compare_select_fusion.1, bf16[864]{0:T(1024)(128)(2,1)} %param.13, bf16[]{:T(256)} %constant.23.clone.1), kind=kCustom, calls=%fused_computation.86 | custom fusion | bytes 2240 | tf_op jit(solution)/shard_map/scatter | solution.py:78
  40.4 5.7 all-to-all-start.4
  57.4 6.5 scatter_custom_fusion.5
  65.0 5.7 all-to-all-start.3
  70.7 20.9 %scatter_custom_fusion.1 = bf16[864,5120]{1,0:T(8,128)(2,1)} fusion(s32[864]{0:T(1024)S(1)} %compare_select_fusion.1, bf16[864,5120]{1,0:T(8,128)(2,1)} %param.10, bf16[]{:T(256)} %constant.23.clone.1), kind=kCustom, calls=%fused_computation.10 | custom fusion | bytes 8847872 | tf_op jit(solution)/shard_map/scatter | solution.py:75
  91.5 8.0 %all_to_all.39 = bf16[8,108,5120]{2,1,0:T(8,128)(2,1)} reshape(bf16[864,5120]{1,0:T(8,128)(2,1)} %scatter_custom_fusion.1) | data formatting | bytes 17694720 | tf_op jit(solution)/shard_map/all_to_all | solution.py:81
  99.5 5.6 all-to-all-start.1
  105.5 5.3 scatter_custom_fusion.9
  111.5 149.6 %all-reduce.1 = (f32[]{:T(128)}, f32[]{:T(128)}) all-reduce(f32[]{:T(128)} %get-tuple-element.4, f32[]{:T(128)} %get-tuple-element.3), channel_id=1, replica_groups=mesh['dp'=8,'shard'=16] {'dp','shard'}, use_global_device_ids=true, to_apply=%region_15.16 | all-reduce | flops 2 | bytes 16 | tf_op jit(solution)/shard_map/psum | solution.py:115
  261.1 5.3 scatter_custom_fusion.4
  266.4 5.3 scatter_custom_fusion.8
  272.5 6.3 scatter_custom_fusion.6
  278.8 8.0 %reshape.71 = bf16[864,5120]{1,0:T(8,128)(2,1)} reshape(bf16[8,108,5120]{2,1,0:T(8,128)(2,1)} %all-to-all-done.1) | data formatting | bytes 17694720 | tf_op jit(solution)/shard_map/all_to_all | solution.py:81
  286.8 19.4 %scatter_custom_fusion.2 = bf16[576,5120]{1,0:T(8,128)(2,1)} fusion(s32[864]{0:T(1024)S(1)} %fusion.48, bf16[864,5120]{1,0:T(8,128)(2,1)} %reshape.71, bf16[]{:T(256)} %constant.23.clone.1), kind=kCustom, calls=%fused_computation.12 | custom fusion | bytes 5898752 | tf_op jit(solution)/shard_map/scatter | solution.py:88
  306.2 5.3 fusion.21
  311.5 5.6 fusion.8
  317.2 109.9 %reduce-scatter.3.cloned.1.call-done = f32[320,512]{1,0:T(8,128)} async-done(((f32[5120,512]{1,0:T(8,128)}), f32[320,512]{1,0:T(8,128)}) %reduce-scatter.3.cloned.1.call-update) | async-done | bytes 655376 | tf_op jit(solution)/shard_map/reduce_scatter | solution.py:125
  427.2 77.0 %all-reduce.5.cloned.1.call-done = f32[320,512]{1,0:T(8,128)} async-done(((f32[320,512]{1,0:T(8,128)}), f32[320,512]{1,0:T(8,128)}) %all-reduce.5.cloned.1.call-update) | async-done | bytes 655376 | tf_op jit(solution)/shard_map/psum | solution.py:128
  507.3 59.0 %all-gather.5.cloned.1.call-done = bf16[5120,512]{1,0:T(8,128)(2,1)} async-done(((bf16[320,512]{1,0:T(8,128)(2,1)}), bf16[5120,512]{1,0:T(8,128)(2,1)}) %all-gather.5.cloned.1.call-update) | async-done | bytes 5242896 | tf_op jit(solution)/shard_map/all_gather | solution.py:120
  571.5 7.7 fusion.4
  579.3 110.0 %reduce-scatter.5.cloned.1.call-done = f32[320,512]{1,0:T(8,128)} async-done(((f32[5120,512]{1,0:T(8,128)}), f32[320,512]{1,0:T(8,128)}) %reduce-scatter.5.cloned.1.call-update) | async-done | bytes 655376 | tf_op jit(solution)/shard_map/reduce_scatter | solution.py:125
  689.3 76.9 %all-reduce.7.cloned.1.call-done = f32[320,512]{1,0:T(8,128)} async-done(((f32[320,512]{1,0:T(8,128)}), f32[320,512]{1,0:T(8,128)}) %all-reduce.7.cloned.1.call-update) | async-done | bytes 655376 | tf_op jit(solution)/shard_map/psum | solution.py:128
  (67 shorter events, 32.9 us)
Async XLA Ops:
  7.2 299.0 %all-gather.3.cloned.1.call-start = ((), (), s32[]{:S(2)}) async-start(), calls=%async_computation.7 | async-start | bytes 5570560 | tf_op jit(solution)/shard_map/all_gather | solution.py:120
  23.9 16.5 %all-to-all-start.2 = ((bf16[8,108,1]{1,2,0:T(2,128)(2,1)}), bf16[8,108,1]{1,2,0:T(2,128)(2,1)S(1)}, u32[]{:S(2)}, u32[]{:S(2)}) async-start(bf16[8,108,1]{1,2,0:T(2,128)(2,1)} %all_to_all.49), calls=%async_computation.2 | async-start | bytes 8192 | tf_op jit(solution)/shard_map/all_to_all | solution.py:83
  40.4 11.8 %all-to-all-start.4 = ((bf16[8,108,1]{1,2,0:T(2,128)(2,1)}), bf16[8,108,1]{1,2,0:T(2,128)(2,1)S(1)}, u32[]{:S(2)}, u32[]{:S(2)}) async-start(bf16[8,108,1]{1,2,0:T(2,128)(2,1)} %all_to_all.50), calls=%async_computation.4 | async-start | bytes 8192 | tf_op jit(solution)/shard_map/all_to_all | solution.py:84
  52.2 12.8 %all-to-all-start = ((s32[8,108,2]{1,2,0:T(2,128)}), s32[8,108,2]{1,2,0:T(2,128)S(1)}, u32[]{:S(2)}, u32[]{:S(2)}) async-start(s32[8,108,2]{1,2,0:T(2,128)} %copy.25), calls=%async_computation | async-start | bytes 16384 | tf_op jit(solution)/shard_map/all_to_all | solution.py:85
  65.0 34.6 %all-to-all-start.3 = ((bf16[8,108,512]{2,1,0:T(8,128)(2,1)}), bf16[8,108,512]{2,1,0:T(8,128)(2,1)S(1)}, u32[]{:S(2)}, u32[]{:S(2)}) async-start(bf16[8,108,512]{2,1,0:T(8,128)(2,1)} %all_to_all.44), calls=%async_computation.3 | async-start | bytes 1835008 | tf_op jit(solution)/shard_map/all_to_all | solution.py:82
  99.5 179.2 %all-to-all-start.1 = ((bf16[8,108,5120]{2,1,0:T(8,128)(2,1)}), bf16[8,108,5120]{2,1,0:T(8,128)(2,1)}, u32[]{:S(2)}, u32[]{:S(2)}) async-start(bf16[8,108,5120]{2,1,0:T(8,128)(2,1)} %all_to_all.39), calls=%async_computation.1 | async-start | bytes 18350080 | tf_op jit(solution)/shard_map/all_to_all | solution.py:81
  105.2 322.0 %reduce-scatter.3.cloned.1.call-start = ((), (), s32[]{:S(2)}) async-start(), calls=%async_computation.8 | async-start | bytes 11141120 | tf_op jit(solution)/shard_map/reduce_scatter | solution.py:125
  306.2 5.3 copy-start
  317.1 187.1 %copy-start.1 = (f32[320,512]{1,0:T(8,128)S(1)}, f32[320,512]{1,0:T(8,128)}, u32[]{:S(2)}) copy-start(f32[320,512]{1,0:T(8,128)} %param.19) | copy-start | bytes 1966084
  317.1 187.1 %copy-start.2 = (f32[320,512]{1,0:T(8,128)S(1)}, f32[320,512]{1,0:T(8,128)}, u32[]{:S(2)}) copy-start(f32[320,512]{1,0:T(8,128)} %param.18) | copy-start | bytes 1966084
  317.1 187.1 %copy-start.4 = (f32[320,512]{1,0:T(8,128)S(1)}, f32[320,512]{1,0:T(8,128)}, u32[]{:S(2)}) copy-start(f32[320,512]{1,0:T(8,128)} %param.17) | copy-start | bytes 1966084
  317.2 187.0 %all-reduce.5.cloned.1.call-start = ((), (), s32[]{:S(2)}) async-start(), calls=%async_computation.9 | async-start | bytes 1310720 | tf_op jit(solution)/shard_map/psum | solution.py:128
  427.2 139.1 %all-gather.5.cloned.1.call-start = ((), (), s32[]{:S(2)}) async-start(), calls=%async_computation.10 | async-start | bytes 5570560 | tf_op jit(solution)/shard_map/all_gather | solution.py:120
  506.6 182.7 %reduce-scatter.5.cloned.1.call-start = ((), (), s32[]{:S(2)}) async-start(), calls=%async_computation.11 | async-start | bytes 11141120 | tf_op jit(solution)/shard_map/reduce_scatter | solution.py:125
  579.2 187.0 %copy-start.3 = (f32[320,512]{1,0:T(8,128)S(1)}, f32[320,512]{1,0:T(8,128)}, u32[]{:S(2)}) copy-start(f32[320,512]{1,0:T(8,128)} %all-reduce.5.cloned.1.call-done) | copy-start | bytes 1966084
  579.2 187.0 %all-reduce.7.cloned.1.call-start = ((), (), s32[]{:S(2)}) async-start(), calls=%async_computation.12 | async-start | bytes 1310720 | tf_op jit(solution)/shard_map/psum | solution.py:128
Sparse Core Ops, SparseCore 0:
  11.0 62.2 all-gather.2
  317.3 109.8 reduce-scatter.2
  429.6 74.5 all-reduce.4
  507.1 59.1 all-gather.4
  579.3 109.8 reduce-scatter.4
  691.6 74.5 all-reduce.6
where the time goes:
time: 785 us; the launch traced here: 776 us
  waiting for transfers between devices  434 us (55%)
  blocking collectives  150 us (19%)
  local copies, waits for them, and re-layouts  112 us (14%)
  starting transfers between devices  28.8 us (4%)
  matrix products  23.8 us (3%)
  between operations  16.4 us (2%)
  other arithmetic  12.2 us (2%)
    reduce_scatter x2, waiting for transfers between devices, body(): lax.psum_scatter(grad_columns(inputs_now, scaled), 'shard', scatter_dimen...  220 us
    psum x2, waiting for transfers between devices, body(): gradient = lax.psum(gradient, 'dp')  154 us
    psum x1, blocking collectives, body(): total = jnp.maximum(lax.psum(local_counts[update], ('dp', 'shard')), 1.0)  150 us
    all_gather x2, waiting for transfers between devices, body(): lax.all_gather(compute_weight, 'shard', axis=0, tiled=True)  59 us
    scatter x1, local copies, waits for them, and re-layouts, body(): send_states = jnp.zeros_like(states).at[send_pos].set(states, mode='drop')  20.9 us
    scatter x1, local copies, waits for them, and re-layouts, body(): jnp.zeros((BAL, width), jnp.bfloat16).at[target_slot]  19.4 us
    all_to_all x2, local copies, waits for them, and re-layouts, body(): lax.all_to_all(send_states, 'dp', split_axis=0, concat_axis=0, tiled=True)  16 us
  transfers between devices with their start and end apart: 11, of which 6 were waited for; matrix products, arithmetic and copies ran while one was open for 14% of the time, Pallas kernels for 0%

commit v1 on v0

v1 whole, which is shorter than its diff:
```python
import jax
import jax.numpy as jnp
from jax import lax
from jax.experimental import pallas as pl
from jax.experimental.pallas import tpu as pltpu
from jax.sharding import PartitionSpec as P

MESH = pl.DeviceIdType.MESH

BAL = 576
UPDATES = 2
PRIOR_STEPS = 100
MB = 288
ROWS = 864
KPAD = 896
D = 5120
VW = 512
PIECE = 160
LANES = 128
ROW_TILE = 288

BETA_ONE = 0.9
BETA_TWO = 0.999
LEARN_RATE = 0.001
DECAY_RATE = 0.01
ADAM_EPS = 1e-08
CLIP_EPS = 0.2

PARTS = ((0, 64), (64, 48), (112, 48))
SUM_TYPES = (jnp.float32, jnp.bfloat16)
N_SUMS = 17
CHUNKS_IN = (0, 1, 3, 2)
CHUNKS_OUT = (2, 1, 3, 0)


def adam_step(master, moment_one, moment_two, gradient, step_num):
    moment_one = BETA_ONE * moment_one + (1.0 - BETA_ONE) * gradient
    moment_two = BETA_TWO * moment_two + (1.0 - BETA_TWO) * gradient * gradient
    first_hat = moment_one / (1.0 - BETA_ONE**step_num)
    second_hat = moment_two / (1.0 - BETA_TWO**step_num)
    master = master - LEARN_RATE * (
        first_hat / (jnp.sqrt(second_hat) + ADAM_EPS) + DECAY_RATE * master
    )
    return (master, moment_one, moment_two)


class Sems:
    def __init__(self, send, recv):
        self.send, self.recv, self.index = send, recv, {}

    def pair(self, *name):
        slot = self.index.setdefault(name, len(self.index))
        return self.send.at[slot], self.recv.at[slot]


N_SEMS = 160


def f32(value):
    return value.astype(jnp.float32)


def kernel(
    states_hbm, read_hbm, meta_ref, w_ref, m_ref, v_ref,
    wo_ref, mo_ref, vo_ref,
    st, st_t, rd, wh, acc, sc, gfull, cnt, cnt_in, load_sem, send_sem, recv_sem, *sums,
):
    dp, sh = lax.axis_index("dp"), lax.axis_index("shard")
    xl, z = dp // 4, dp % 4
    y, xh, c = sh // 4, (sh // 2) % 2, sh % 2
    x = xh * 2 + xl

    def device(x_, y_, z_, c_):
        return ((x_ % 2) * 4 + z_, y_ * 4 + (x_ // 2) * 2 + c_)

    def turn(axis, d):
        return ({"x": x, "y": y, "z": z}[axis] + d) % 4

    def peer(axis, d):
        to = turn(axis, d)
        return device(
            to if axis == "x" else x, to if axis == "y" else y, to if axis == "z" else z, c
        )

    twin = device(x, y, z, 1 - c)
    partner = device(xh * 2 + (1 - xl), y, z, c)

    def lanes(index):
        return pl.ds(pl.multiple_of(index * LANES, LANES), LANES)

    zc = lanes(z)
    rows_of = [pl.ds(first, size) for first, size in PARTS]
    sems = Sems(send_sem, recv_sem)

    def send(src, dst, to, *name):
        send_at, recv_at = sems.pair(*name)
        copy = pltpu.make_async_remote_copy(
            src_ref=src, dst_ref=dst, send_sem=send_at, recv_sem=recv_at,
            device_id=to, device_id_type=MESH,
        )
        copy.start()
        return copy

    loads = []
    for k in range(4):
        cols = pl.ds(k * 1280, 1280)
        loads.append(pltpu.make_async_copy(states_hbm.at[:, cols], st.at[:, cols], load_sem.at[k]))
    loads.append(pltpu.make_async_copy(read_hbm, rd, load_sem.at[4]))
    for load in loads:
        load.start()

    barrier = pltpu.get_barrier_semaphore()
    greeted = [peer(axis, d) for axis in "xyz" for d in (1, 2, 3)] + [twin]
    for to in greeted:
        pl.semaphore_signal(barrier, inc=1, device_id=to, device_id_type=MESH)

    own_rows = pl.ds(pl.multiple_of(xl * PIECE, PIECE), PIECE)
    wh[c, y, x, :, zc] = w_ref[own_rows, zc].astype(jnp.bfloat16)
    lane = lax.broadcasted_iota(jnp.int32, (8, LANES), 1)
    cnt[...] = jnp.where(
        lane == 0,
        jnp.sum(meta_ref[:, 2:3], axis=0, keepdims=True),
        jnp.where(lane == 1, jnp.sum(meta_ref[:, 3:4], axis=0, keepdims=True), 0.0),
    )
    sc[pl.ds(ROWS, KPAD - ROWS), :] = jnp.zeros((KPAD - ROWS, VW), jnp.bfloat16)
    pl.semaphore_wait(barrier, len(greeted))

    def count_start(stage, axis):
        return [
            send(cnt, cnt_in.at[stage, d - 1], peer(axis, d), "cnt", stage, d) for d in (1, 2, 3)
        ]

    def count_end(stage, copies):
        for copy in copies:
            copy.wait()
        total = cnt[...]
        for d in range(3):
            total = total + cnt_in[stage, d]
        cnt[...] = total

    def transpose_chunk(k):
        loads[k].wait()

        def step(j, carry):
            cols = pl.ds(pl.multiple_of(k * 1280 + j * LANES, LANES), LANES)
            block = jnp.concatenate(
                [st[:, cols], jnp.zeros((KPAD - ROWS, LANES), jnp.bfloat16)], axis=0
            )
            st_t[cols, :] = block.T
            return carry

        lax.fori_loop(0, 10, step, 0)

    def fwd_chunk(yy, first):
        def step(i, carry):
            rows = pl.ds(pl.multiple_of(i * ROW_TILE, ROW_TILE), ROW_TILE)
            weight = jnp.concatenate(
                [
                    wh[core, yy, pl.ds(2 * half, 2)].reshape(2 * PIECE, VW)
                    for half in (0, 1)
                    for core in (0, 1)
                ],
                axis=0,
            )
            cols = pl.ds(pl.multiple_of(yy * 1280, 1280), 1280)
            proj = jnp.dot(st[rows, cols], weight, preferred_element_type=jnp.float32)
            prod = proj * f32(rd[rows, :])
            part = (
                prod[:, 0:128] + prod[:, 128:256] + prod[:, 256:384] + prod[:, 384:512]
            )
            if first:
                acc[rows, :] = part
            else:
                acc[rows, :] += part
            return carry

        lax.fori_loop(0, ROWS // ROW_TILE, step, 0)

    def scale_rows(u):
        total = jnp.maximum(cnt[0:1, u : u + 1], 1.0)

        def step(i, carry):
            rows = pl.ds(pl.multiple_of(i * ROW_TILE, ROW_TILE), ROW_TILE)
            shift, adv = meta_ref[rows, 0:1], meta_ref[rows, 1:2]
            weights = meta_ref[rows, 2 + u : 3 + u]
            log_ratio = shift + jnp.sum(acc[rows, :], axis=1, keepdims=True)
            ratio = jnp.exp(log_ratio)
            clipped = jnp.clip(ratio, 1.0 - CLIP_EPS, 1.0 + CLIP_EPS)
            chosen = ratio * adv <= clipped * adv
            coeff = jnp.where(
                (weights > 0.0) & chosen, -(weights / total) * adv * ratio, 0.0
            )
            sc[rows, :] = (coeff * f32(rd[rows, :])).astype(jnp.bfloat16)
            return carry

        lax.fori_loop(0, ROWS // ROW_TILE, step, 0)

    def grad_half(core, yy, half):
        first = pl.multiple_of(yy * 1280 + half * 640 + core * 320, 320)
        return jnp.dot(
            st_t[pl.ds(first, 320), :], sc[...], preferred_element_type=jnp.float32
        )

    for u in range(UPDATES):
        sent = []
        first_axes, second_axes = "zxy", "xyz"
        hop = {}
        for p in range(3):
            block = wh.at[c, y, x, rows_of[p], zc]
            hop[p] = [
                send(block, block, peer(first_axes[p], d), "ag1", p, d) for d in (1, 2, 3)
            ]
            sent += hop[p]
        if u == 0:
            counting = count_start(0, "z")
            transpose_chunk(0)
        for p in range(3):
            for copy in hop[p]:
                copy.wait_recv()
            block = (
                wh.at[c, y, x, rows_of[p], :],
                wh.at[c, y, :, rows_of[p], zc],
                wh.at[c, :, x, rows_of[p], zc],
            )[p]
            hop[p] = [
                send(block, block, peer(second_axes[p], d), "ag2", p, d) for d in (1, 2, 3)
            ]
            sent += hop[p]
        if u == 0:
            count_end(0, counting)
            counting = count_start(1, "x")
            transpose_chunk(1)
        for p in range(3):
            for copy in hop[p]:
                copy.wait_recv()
        arrive = {o: [] for o in CHUNKS_IN}
        for o in CHUNKS_IN:
            yy = (y + o) % 4
            if o == 0:
                block = wh.at[c, y, :, rows_of[0], :]
                for d in (1, 3, 2):
                    arrive[(4 - d) % 4].append(send(block, block, peer("y", d), "ag3", 0, d))
            block = wh.at[c, yy, :, rows_of[1], zc]
            arrive[o] += [
                send(block, block, peer("z", d), "ag3", 1, o, d) for d in (1, 2, 3)
            ]
            block = wh.at[c, yy, x, rows_of[2], :]
            arrive[o] += [
                send(block, block, peer("x", d), "ag3", 2, o, d) for d in (1, 2, 3)
            ]
        if u == 0:
            count_end(1, counting)
            counting = count_start(2, "y")
            transpose_chunk(2)
            transpose_chunk(3)
            count_end(2, counting)
            counting = [send(cnt, cnt_in.at[3, 0], twin, "cnt", 3)]
            loads[4].wait()
        else:
            block = gfull.at[0, own_rows, zc]
            shared = [send(block, block, peer("z", d), "gz", 0, d) for d in (1, 2, 3)]
            crossed = send(block, block, partner, "gx", 0)

        across = {}
        for i, o in enumerate(CHUNKS_IN):
            ahead = CHUNKS_IN[: 2] if i == 0 else CHUNKS_IN[i + 1 : i + 2]
            for a in ahead:
                for copy in arrive[a]:
                    copy.wait_recv()
                    sent.append(copy)
                block = wh.at[c, (y + a) % 4]
                across[a] = send(block, block, twin, "agc", a)
            across[o].wait_recv()
            fwd_chunk((y + o) % 4, i == 0)
        if u == 0:
            counting[0].wait()
            cnt[...] = cnt[...] + cnt_in[3, 0]
        else:
            crossed.wait()
            block = gfull.at[0, pl.ds(pl.multiple_of((1 - xl) * PIECE, PIECE), PIECE), zc]
            shared += [send(block, block, peer("z", d), "gy", 0, d) for d in (1, 2, 3)]
        scale_rows(u)
        for copy in sent:
            copy.wait_send()
        for o in CHUNKS_IN:
            across[o].wait_send()

        sent = []
        kind = SUM_TYPES[u]
        gsend, gs, r0, r1, r2, s0, s1, s2, q0, q1, q2, t0, t1, t2, e0, e1, e2 = sums[
            N_SUMS * u : N_SUMS * (u + 1)
        ]

        def give(i, given):
            yy = (y + CHUNKS_OUT[i]) % 4
            if i >= 2:
                given[i - 2].wait_send()
            for half in (0, 1):
                gsend[i % 2, pl.ds(2 * half, 2)] = (
                    grad_half(1 - c, yy, half).astype(kind).reshape(2, PIECE, VW)
                )
            given.append(send(gsend.at[i % 2], gs.at[yy], twin, "rsc", i))

        def keep(i, given):
            yy = (y + CHUNKS_OUT[i]) % 4
            given[i].wait_recv()
            for half in (0, 1):
                other = gs[yy, pl.ds(2 * half, 2)].reshape(2 * PIECE, VW)
                gs[yy, pl.ds(2 * half, 2)] = (
                    (grad_half(c, yy, half) + f32(other)).astype(kind).reshape(2, PIECE, VW)
                )

        def first_sends(o):
            yy = (y + o) % 4
            out = {0: [], 1: [], 2: []}
            if o:
                out[0].append(
                    send(gs.at[yy, :, rows_of[0], :], r0.at[o - 1], peer("y", o), "rs1", 0, o)
                )
            for d in (1, 2, 3):
                out[1].append(
                    send(
                        gs.at[yy, :, rows_of[1], lanes(turn("z", d))], r1.at[d - 1, yy],
                        peer("z", d), "rs1", 1, o, d,
                    )
                )
                out[2].append(
                    send(
                        gs.at[yy, turn("x", d), rows_of[2], :], r2.at[d - 1, yy],
                        peer("x", d), "rs1", 2, o, d,
                    )
                )
            return out

        def add_up(own, parts):
            total = f32(own)
            for part in parts:
                total = total + f32(part)
            return total

        def first_sums(o, out):
            yy = (y + o) % 4
            for copy in out[1] + out[2]:
                copy.wait_recv()
            s1[yy] = add_up(gs[yy, :, rows_of[1], zc], [r1[d, yy] for d in range(3)]).astype(kind)
            s2[yy] = add_up(gs[yy, x, rows_of[2], :], [r2[d, yy] for d in range(3)]).astype(kind)

        given = []
        give(0, given)
        outs = {}
        for i, o in enumerate(CHUNKS_OUT):
            if i + 1 < 4:
                give(i + 1, given)
            keep(i, given)
            outs[o] = first_sends(o)
            if i:
                first_sums(CHUNKS_OUT[i - 1], outs[CHUNKS_OUT[i - 1]])
        for o in (1, 2, 3):
            outs[o][0][0].wait_recv()
        for xx in range(4):
            s0[xx] = add_up(gs[y, xx, rows_of[0], :], [r0[d, xx] for d in range(3)]).astype(kind)
        hop = {0: [], 1: [], 2: []}
        for d in (1, 2, 3):
            hop[0].append(send(s0.at[turn("x", d)], q0.at[d - 1], peer("x", d), "rs2", 0, d))
        first_sums(CHUNKS_OUT[3], outs[CHUNKS_OUT[3]])
        for d in (1, 2, 3):
            hop[1].append(send(s1.at[turn("y", d)], q1.at[d - 1], peer("y", d), "rs2", 1, d))
            hop[2].append(
                send(s2.at[:, :, lanes(turn("z", d))], q2.at[d - 1], peer("z", d), "rs2", 2, d)
            )
        for o in CHUNKS_OUT:
            sent += outs[o][0] + outs[o][1] + outs[o][2]
        sent += given[2:]
        for p in range(3):
            for copy in hop[p]:
                copy.wait_recv()
            sent += hop[p]
            hop[p] = []
            if p == 0:
                t0[...] = add_up(s0[x], [q0[d] for d in range(3)]).astype(kind)
                for d in (1, 2, 3):
                    hop[0].append(
                        send(t0.at[:, lanes(turn("z", d))], e0.at[d - 1], peer("z", d), "rs3", 0, d)
                    )
            elif p == 1:
                t1[...] = add_up(s1[y], [q1[d] for d in range(3)]).astype(kind)
                for d in (1, 2, 3):
                    hop[1].append(
                        send(t1.at[turn("x", d)], e1.at[d - 1], peer("x", d), "rs3", 1, d)
                    )
            else:
                t2[...] = add_up(s2[:, :, zc], [q2[d] for d in range(3)]).astype(kind)
                for d in (1, 2, 3):
                    hop[2].append(
                        send(t2.at[turn("y", d)], e2.at[d - 1], peer("y", d), "rs3", 2, d)
                    )
        for p in range(3):
            for copy in hop[p]:
                copy.wait_recv()
            sent += hop[p]
        gradient = jnp.concatenate(
            [
                add_up(t0[:, zc], [e0[d] for d in range(3)]),
                add_up(t1[x], [e1[d] for d in range(3)]),
                add_up(t2[y], [e2[d] for d in range(3)]),
            ],
            axis=0,
        )
        gfull[u, own_rows, zc] = gradient
        if u == 0:
            master, _, _ = adam_step(
                w_ref[own_rows, zc], m_ref[own_rows, zc], v_ref[own_rows, zc],
                gradient, PRIOR_STEPS + 1,
            )
            wh[c, y, x, :, zc] = master.astype(jnp.bfloat16)
        else:
            block = gfull.at[1, own_rows, zc]
            last = [send(block, block, partner, "gx", 1)]
            shared += [send(block, block, peer("z", d), "gz", 1, d) for d in (1, 2, 3)]
            last[0].wait_recv()
            block = gfull.at[1, pl.ds(pl.multiple_of((1 - xl) * PIECE, PIECE), PIECE), zc]
            shared += [send(block, block, peer("z", d), "gy", 1, d) for d in (1, 2, 3)]
            for copy in shared:
                copy.wait_recv()
            sent += shared + last
        for copy in sent:
            copy.wait_send()

    def finish(i, carry):
        rows = pl.ds(pl.multiple_of(i * 32, 32), 32)
        master, one, two = w_ref[rows, :], m_ref[rows, :], v_ref[rows, :]
        for u in range(UPDATES):
            master, one, two = adam_step(master, one, two, gfull[u, rows, :], PRIOR_STEPS + u + 1)
        wo_ref[rows, :] = master
        mo_ref[rows, :] = one
        vo_ref[rows, :] = two
        return carry

    lax.fori_loop(0, 10, finish, 0)


def body(
    states, readout, logp_shift, advantage, response_mask, rollout_len, dest_slot,
    weight, moment1, moment2,
):
    row_index = jnp.arange(ROWS, dtype=jnp.int32)
    live = (row_index < rollout_len[0]) & (dest_slot >= 0)
    batch = jnp.where(live, (dest_slot % BAL) // MB, UPDATES)
    token = response_mask.astype(jnp.float32)
    meta = jnp.stack(
        [logp_shift.astype(jnp.float32), advantage.astype(jnp.float32)]
        + [jnp.where(batch == k, token, 0.0) for k in range(UPDATES)],
        axis=1,
    )
    bf16, full = jnp.bfloat16, jnp.float32
    vmem = pl.BlockSpec(memory_space=pltpu.VMEM)
    hbm = pl.BlockSpec(memory_space=pl.ANY)
    a, b, d = [size for _, size in PARTS]
    sums = [
        (2, 4, PIECE, VW), (4, 4, PIECE, VW),
        (3, 4, a, VW), (3, 4, 4, b, LANES), (3, 4, d, VW),
        (4, a, VW), (4, 4, b, LANES), (4, d, VW),
        (3, a, VW), (3, 4, b, LANES), (3, 4, d, LANES),
        (a, VW), (4, b, LANES), (4, d, LANES),
        (3, a, LANES), (3, b, LANES), (3, d, LANES),
    ]
    shard = jax.ShapeDtypeStruct(weight.shape, full)
    return pl.pallas_call(
        kernel,
        out_shape=(shard, shard, shard),
        in_specs=[hbm, hbm, vmem, vmem, vmem, vmem],
        out_specs=(vmem, vmem, vmem),
        scratch_shapes=[
            pltpu.VMEM((ROWS, D), bf16),
            pltpu.VMEM((D, KPAD), bf16),
            pltpu.VMEM((ROWS, VW), bf16),
            pltpu.VMEM((2, 4, 4, PIECE, VW), bf16),
            pltpu.VMEM((ROWS, LANES), full),
            pltpu.VMEM((KPAD, VW), bf16),
            pltpu.VMEM((2, 2 * PIECE, VW), full),
            pltpu.VMEM((8, LANES), full),
            pltpu.VMEM((4, 3, 8, LANES), full),
            pltpu.SemaphoreType.DMA((5,)),
            pltpu.SemaphoreType.DMA((N_SEMS,)),
            pltpu.SemaphoreType.DMA((N_SEMS,)),
        ]
        + [pltpu.VMEM(dims, kind) for kind in SUM_TYPES for dims in sums],
        compiler_params=pltpu.CompilerParams(
            collective_id=0, has_side_effects=True, vmem_limit_bytes=58 * 1024 * 1024
        ),
    )(states, readout, meta, weight, moment1, moment2)


def solution(mesh):
    rows = P(("dp", "shard"))
    return jax.shard_map(
        body,
        mesh=mesh,
        in_specs=(
            P(("dp", "shard"), None), P(("dp", "shard"), None), rows, rows, rows, rows, rows,
            P("shard", None), P("shard", None), P("shard", None),
        ),
        out_specs=(P("shard", None), P("shard", None), P("shard", None)),
        check_vma=False,
    )
```

time: 785 us -> 160 us (0.20); the launches traced: 776 us -> 159 us
  waiting for transfers between devices: 434 us -> 0 us
  blocking collectives: 150 us -> 0 us
  Pallas kernels: 0 us -> 149 us
  local copies, waits for them, and re-layouts: 112 us -> 8.25 us
  starting transfers between devices: 28.8 us -> 0 us
  matrix products: 23.8 us -> 0 us
  between operations: 16.4 us -> 1.31 us
  other arithmetic: 12.2 us -> 0.75 us
    reduce_scatter x2 -> x0, waiting for transfers between devices: 220 us -> none  [body(): lax.psum_scatter(grad_columns(inputs_now, scaled), 'shard', scatter_dimen...]
    psum x2 -> x0, waiting for transfers between devices: 154 us -> none  [body(): gradient = lax.psum(gradient, 'dp')]
    psum x1 -> x0, blocking collectives: 150 us -> none  [body(): total = jnp.maximum(lax.psum(local_counts[update], ('dp', 'shard')), 1.0)]
    pallas_call x0 -> x1, Pallas kernels: none -> 149 us  [body(): pl.pallas_call(kernel, out_shape=(shard, shard, shard), in_specs=[hbm, hb...]
    scatter x11 -> x0, local copies, waits for them, and re-layouts: 90.8 us -> none  [the longest x1 20.9 us: body(): send_states = jnp.zeros_like(states).at[send_pos].set(states, mode='drop')]
    all_gather x2 -> x0, waiting for transfers between devices: 59 us -> none  [body(): lax.all_gather(compute_weight, 'shard', axis=0, tiled=True)]
    all_to_all x5 -> x0, starting transfers between devices: 28.5 us -> none  [the longest x1 6.32 us: body(): lax.all_to_all(send_shift, 'dp', split_axis=0, concat_axis=0, tiled=True)]
    dot_general x4 -> x0, matrix products: 23.8 us -> none  [the longest x2 13.3 us: grad_columns(): lax.dot_general(inputs_now, scaled, (((0,), (0,)), ((), ())), preferred_e...]
  transfers between devices with their start and end apart: 11 -> 0, of which waited for: 6 -> 0; matrix products, arithmetic and copies ran while one was open for 14% -> 0% of each run, Pallas kernels for 0% -> 0%
where the time goes in v1:
time: 160 us; the launch traced here: 159 us
  Pallas kernels  149 us (93%)
  local copies, waits for them, and re-layouts  8.25 us (5%)
    pallas_call x1, Pallas kernels, body(): pl.pallas_call(kernel, out_shape=(shard, shard, shard), in_specs=[hbm, hb...  149 us
    unnamed x3, local copies, waits for them, and re-layouts  5.9 us

profile of v1, /device:TPU:0, one launch (start us, length us, event | category | flops | bytes accessed | tf_op | source)
XLA Modules:
  0.0 159.4 jit_solution(13625560829652408733)
XLA Ops:
  1.3 0.7 reshape.6
  2.0 0.7 reshape.7
  2.6 0.7 convert_select_fusion.1
  3.4 1.0 copy.17.meta_ref
  4.4 149.1 %shard_map.121 = (f32[320,512]{1,0:T(8,128)}, f32[320,512]{1,0:T(8,128)}, f32[320,512]{1,0:T(8,128)}) custom-call(bf16[864,5120]{1,0:T(8,128)(2,1)} %states_hbm.1, bf16[864,512]{1,0:T(8,128)(2,1)} %read_hbm.1, f32[864,4]{1,0:T(8,128)} %copy.17.meta_ref, f32[320,512]{1,0:T(8,128)} %w_ref.1, f32[320,512]{1,0:T(8,128)} %m_ref.1, f32[320,512]{1,0:T(8,128)} %v_ref.1), custom_call_target="tpu_custom_call" | custom-call | tf_op jit(solution)/shard_map/pallas_call | solution.py:468
  153.5 2.0 %copy.22 = f32[320,512]{1,0:T(8,128)} copy(f32[320,512]{1,0:T(8,128)} %get-tuple-element.8) | data formatting | bytes 1310720
  155.5 2.0 %copy.23 = f32[320,512]{1,0:T(8,128)} copy(f32[320,512]{1,0:T(8,128)} %get-tuple-element.9) | data formatting | bytes 1310720
  157.5 2.0 %copy.24 = f32[320,512]{1,0:T(8,128)} copy(f32[320,512]{1,0:T(8,128)} %get-tuple-element.10) | data formatting | bytes 1310720
  (3 shorter events, 0.0 us)

commit v2 on v1

v2 whole, which is shorter than its diff:
```python
import jax
import jax.numpy as jnp
from jax import lax
from jax.experimental import pallas as pl
from jax.experimental.pallas import tpu as pltpu
from jax.sharding import PartitionSpec as P

MESH = pl.DeviceIdType.MESH

BAL = 576
UPDATES = 2
PRIOR_STEPS = 100
MB = 288
ROWS = 864
KPAD = 896
D = 5120
VW = 512
PIECE = 160
LANES = 128
ROW_TILE = 288

BETA_ONE = 0.9
BETA_TWO = 0.999
LEARN_RATE = 0.001
DECAY_RATE = 0.01
ADAM_EPS = 1e-08
CLIP_EPS = 0.2

PARTS = ((0, 64), (64, 48), (112, 48))
SUM_TYPES = (jnp.float32, jnp.bfloat16)
N_SUMS = 18
CHUNKS_IN = (0, 1, 3, 2)
CHUNKS_OUT = (2, 1, 3, 0)


def adam_step(master, moment_one, moment_two, gradient, step_num):
    moment_one = BETA_ONE * moment_one + (1.0 - BETA_ONE) * gradient
    moment_two = BETA_TWO * moment_two + (1.0 - BETA_TWO) * gradient * gradient
    first_hat = moment_one / (1.0 - BETA_ONE**step_num)
    second_hat = moment_two / (1.0 - BETA_TWO**step_num)
    master = master - LEARN_RATE * (
        first_hat / (jnp.sqrt(second_hat) + ADAM_EPS) + DECAY_RATE * master
    )
    return (master, moment_one, moment_two)


class Sems:
    def __init__(self, send, recv):
        self.send, self.recv, self.index = send, recv, {}

    def pair(self, *name):
        slot = self.index.setdefault(name, len(self.index))
        return self.send.at[slot], self.recv.at[slot]


N_SEMS = 200


def f32(value):
    return value.astype(jnp.float32)


def kernel(
    states_hbm, read_hbm, meta_ref, w_hbm, m_hbm, v_hbm, out_ref,
    st, st_t, rd, meta, w_ref, m_ref, v_ref, wh, acc, sc, cnt, cnt_in,
    load_sem, send_sem, recv_sem, *sums,
):
    dp, sh = lax.axis_index("dp"), lax.axis_index("shard")
    xl, z = dp // 4, dp % 4
    y, xh, c = sh // 4, (sh // 2) % 2, sh % 2
    x = xh * 2 + xl

    def device(x_, y_, z_, c_):
        return ((x_ % 2) * 4 + z_, y_ * 4 + (x_ // 2) * 2 + c_)

    def turn(axis, d):
        return ({"x": x, "y": y, "z": z}[axis] + d) % 4

    def peer(axis, d):
        to = turn(axis, d)
        return device(
            to if axis == "x" else x, to if axis == "y" else y, to if axis == "z" else z, c
        )

    twin = device(x, y, z, 1 - c)
    pair = xh * 2 + (1 - xl)
    replicas = [device(pair, y, turn("z", d), c) for d in range(4)]
    across_xy = [device(turn("x", 2), turn("y", d), z, c) for d in range(4)]

    def lanes(index):
        return pl.ds(pl.multiple_of(index * LANES, LANES), LANES)

    zc = lanes(z)
    rows_of = [pl.ds(first, size) for first, size in PARTS]
    sems = Sems(send_sem, recv_sem)

    def send(src, dst, to, *name):
        send_at, recv_at = sems.pair(*name)
        copy = pltpu.make_async_remote_copy(
            src_ref=src, dst_ref=dst, send_sem=send_at, recv_sem=recv_at,
            device_id=to, device_id_type=MESH,
        )
        copy.start()
        return copy

    own_rows = pl.ds(pl.multiple_of(xl * PIECE, PIECE), PIECE)

    loads = [pltpu.make_async_copy(w_hbm, w_ref, load_sem.at[0])]
    for k in range(4):
        cols = pl.ds(k * 1280, 1280)
        loads.append(
            pltpu.make_async_copy(states_hbm.at[:, cols], st.at[:, cols], load_sem.at[1 + k])
        )
    loads.append(pltpu.make_async_copy(read_hbm, rd, load_sem.at[5]))
    loads.append(pltpu.make_async_copy(m_hbm.at[own_rows, zc], m_ref, load_sem.at[6]))
    loads.append(pltpu.make_async_copy(v_hbm.at[own_rows, zc], v_ref, load_sem.at[7]))
    for load in loads:
        load.start()

    barrier = pltpu.get_barrier_semaphore()
    greeted = [peer(axis, d) for axis in "xyz" for d in (1, 2, 3)] + [twin]
    greeted += replicas[1:] + across_xy[1:]
    for to in greeted:
        pl.semaphore_signal(barrier, inc=1, device_id=to, device_id_type=MESH)

    meta[...] = meta_ref[...].T
    lane = lax.broadcasted_iota(jnp.int32, (8, LANES), 1)
    cnt[...] = jnp.where(
        lane == 0,
        jnp.sum(meta_ref[2:3, :], axis=1, keepdims=True),
        jnp.where(lane == 1, jnp.sum(meta_ref[3:4, :], axis=1, keepdims=True), 0.0),
    )
    sc[pl.ds(ROWS, KPAD - ROWS), :] = jnp.zeros((KPAD - ROWS, VW), jnp.bfloat16)
    loads[0].wait()
    for p in (0, 2):
        first, size = PARTS[p]
        rows = pl.ds(pl.multiple_of(xl * PIECE + first, 16), size)
        wh[c, y, x, rows_of[p], :] = w_ref[rows, :].astype(jnp.bfloat16)
    for half in range(2):
        first, size = PARTS[1]
        rows = pl.ds(half * PIECE + first, size)
        wh[c, y, 2 * xh + half, rows_of[1], zc] = w_ref[rows, zc].astype(jnp.bfloat16)
    pl.semaphore_wait(barrier, len(greeted))

    def count_start(stage, axis):
        return [
            send(cnt, cnt_in.at[stage, d - 1], peer(axis, d), "cnt", stage, d) for d in (1, 2, 3)
        ]

    def count_end(stage, copies):
        for copy in copies:
            copy.wait()
        total = cnt[...]
        for d in range(3):
            total = total + cnt_in[stage, d]
        cnt[...] = total

    def transpose_chunk(k):
        loads[1 + k].wait()

        def step(j, carry):
            cols = pl.ds(pl.multiple_of(k * 1280 + j * LANES, LANES), LANES)
            block = jnp.concatenate(
                [st[:, cols], jnp.zeros((KPAD - ROWS, LANES), jnp.bfloat16)], axis=0
            )
            st_t[cols, :] = block.T
            return carry

        lax.fori_loop(0, 10, step, 0)

    def fwd_chunk(yy, first):
        def step(i, carry):
            rows = pl.ds(pl.multiple_of(i * ROW_TILE, ROW_TILE), ROW_TILE)
            weight = jnp.concatenate(
                [
                    wh[core, yy, pl.ds(2 * half, 2)].reshape(2 * PIECE, VW)
                    for half in (0, 1)
                    for core in (0, 1)
                ],
                axis=0,
            )
            cols = pl.ds(pl.multiple_of(yy * 1280, 1280), 1280)
            proj = jnp.dot(st[rows, cols], weight, preferred_element_type=jnp.float32)
            prod = proj * f32(rd[rows, :])
            part = (
                prod[:, 0:128] + prod[:, 128:256] + prod[:, 256:384] + prod[:, 384:512]
            )
            if first:
                acc[rows, :] = part
            else:
                acc[rows, :] += part
            return carry

        lax.fori_loop(0, ROWS // ROW_TILE, step, 0)

    def scale_rows(u):
        total = jnp.maximum(cnt[0:1, u : u + 1], 1.0)

        def step(i, carry):
            rows = pl.ds(pl.multiple_of(i * ROW_TILE, ROW_TILE), ROW_TILE)
            shift, adv = meta[rows, 0:1], meta[rows, 1:2]
            weights = meta[rows, 2 + u : 3 + u]
            log_ratio = shift + jnp.sum(acc[rows, :], axis=1, keepdims=True)
            ratio = jnp.exp(log_ratio)
            clipped = jnp.clip(ratio, 1.0 - CLIP_EPS, 1.0 + CLIP_EPS)
            chosen = ratio * adv <= clipped * adv
            coeff = jnp.where(
                (weights > 0.0) & chosen, -(weights / total) * adv * ratio, 0.0
            )
            sc[rows, :] = (coeff * f32(rd[rows, :])).astype(jnp.bfloat16)
            return carry

        lax.fori_loop(0, ROWS // ROW_TILE, step, 0)

    def grad_half(core, yy, half):
        first = pl.multiple_of(yy * 1280 + half * 640 + core * 320, 320)
        return jnp.dot(
            st_t[pl.ds(first, 320), :], sc[...], preferred_element_type=jnp.float32
        )

    def add_up(own, parts):
        total = f32(own)
        for part in parts:
            total = total + f32(part)
        return total

    def share(u):
        block = out_ref.at[u, own_rows, zc]
        return [send(block, block, peer("z", d), "share", u, 0, d) for d in (1, 2, 3)] + [
            send(block, block, replicas[d], "share", u, 1, d) for d in range(4)
        ]

    shared = []
    for u in range(UPDATES):
        sent = []

        def ring(axis, block, *name):
            copies = [send(block, block, peer(axis, d), *name, d) for d in (1, 3, 2)]
            sent.extend(copies)
            return dict(zip((1, 3, 2), copies))

        def along_y(j):
            block = wh.at[c, y, turn("x", -j), rows_of[0], :]
            return {d: send(block, block, peer("y", d), "ag3", 0, j, d) for d in (1, 3)}

        whole = wh.at[c, y, x, rows_of[0], :]
        part_y, part_z, part_x = {}, {}, {}
        if u == 0:
            second = {0: ring("x", whole, "ag2", 0)}
            both = wh.at[c, y, pl.ds(2 * xh, 2), rows_of[1], zc]
            plane = [send(both, both, across_xy[0], "ag2", 1, 0)]
            plane += [send(both, both, peer("y", d), "ag2", 1, 1, d) for d in (1, 2, 3)]
            plane += [send(both, both, across_xy[d], "ag2", 1, 2, d) for d in (1, 2, 3)]
            sent += plane
            second[2] = ring("y", wh.at[c, y, x, rows_of[2], :], "ag2", 2)
            part_y[0] = along_y(0)
            counting = count_start(0, "z")
            transpose_chunk(0)
            count_end(0, counting)
            counting = count_start(1, "x")
            for copy in plane:
                copy.wait_recv()
            part_z[0] = ring("z", wh.at[c, y, :, rows_of[1], zc], "ag3", 1, 0)
        else:
            first = [
                ring(axis, wh.at[c, y, x, rows_of[p], zc], "ag1", p)
                for p, axis in enumerate("zxy")
            ]
            second = {}
            for copy in first[0].values():
                copy.wait_recv()
            second[0] = ring("x", whole, "ag2", 0)
            for copy in first[1].values():
                copy.wait_recv()
            second[1] = ring("y", wh.at[c, y, :, rows_of[1], zc], "ag2", 1)
            for copy in first[2].values():
                copy.wait_recv()
            second[2] = ring("z", wh.at[c, :, x, rows_of[2], zc], "ag2", 2)
            part_y[0] = along_y(0)
            part_z[0] = ring("z", wh.at[c, y, :, rows_of[1], zc], "ag3", 1, 0)
        for d in (1, 3):
            second[0][d].wait_recv()
            part_y[d] = along_y(d)
        if u == 1:
            for copy in second[2].values():
                copy.wait_recv()
        part_x[0] = ring("x", wh.at[c, y, x, rows_of[2], :], "ag3", 2, 0)
        second[0][2].wait_recv()
        part_y[2] = along_y(2)
        for o in (1, 3, 2):
            yy = (y + o) % 4
            if u == 1:
                second[1][4 - o].wait_recv()
            part_z[o] = ring("z", wh.at[c, yy, :, rows_of[1], zc], "ag3", 1, o)
            if u == 0:
                second[2][4 - o].wait_recv()
            part_x[o] = ring("x", wh.at[c, yy, x, rows_of[2], :], "ag3", 2, o)
        if u == 0:
            transpose_chunk(1)
            count_end(1, counting)
            counting = count_start(2, "y")

        relays = []
        for j, d in ((0, 1), (1, 1), (3, 3), (2, 3)):
            part_y[j][d].wait_recv()
            block = wh.at[c, turn("y", -d), turn("x", -j), rows_of[0], :]
            relays.append(send(block, block, peer("y", d), "ag4", j))

        def arrived(o):
            if o == 2:
                for copy in relays:
                    copy.wait_recv()
            elif o:
                for j in range(4):
                    if (j, 4 - o) not in ((0, 1), (1, 1), (3, 3), (2, 3)):
                        part_y[j][4 - o].wait_recv()
            for copy in list(part_z[o].values()) + list(part_x[o].values()):
                copy.wait_recv()

        if u == 0:
            transpose_chunk(2)
            transpose_chunk(3)
            count_end(2, counting)
            counting = [send(cnt, cnt_in.at[3, 0], twin, "cnt", 3)]
            loads[5].wait()
        across = {}
        for i, o in enumerate(CHUNKS_IN):
            for a in CHUNKS_IN[:2] if i == 0 else CHUNKS_IN[i + 1 : i + 2]:
                arrived(a)
                block = wh.at[c, (y + a) % 4]
                across[a] = send(block, block, twin, "agc", a)
                if u == 1 and a == CHUNKS_IN[3]:
                    shared += share(0)
            across[o].wait_recv()
            fwd_chunk((y + o) % 4, i == 0)
        if u == 0:
            counting[0].wait()
            cnt[...] = cnt[...] + cnt_in[3, 0]
        scale_rows(u)
        for j in range(4):
            sent += part_y[j].values()
        sent += relays
        sent += across.values()
        for copy in sent:
            copy.wait_send()

        sent = []
        kind = SUM_TYPES[u]
        gsend, gs, rel, r0, r1, r2, s0, s1, s2, q0, q1, q2, t0, t1, t2, e0, e1, e2 = sums[
            N_SUMS * u : N_SUMS * (u + 1)
        ]

        def give(i, given):
            yy = (y + CHUNKS_OUT[i]) % 4
            if i >= 2:
                given[i - 2].wait_send()
            for half in (0, 1):
                gsend[i % 2, pl.ds(2 * half, 2)] = (
                    grad_half(1 - c, yy, half).astype(kind).reshape(2, PIECE, VW)
                )
            given.append(send(gsend.at[i % 2], gs.at[yy], twin, "rsc", i))

        def keep(i, given):
            yy = (y + CHUNKS_OUT[i]) % 4
            given[i].wait_recv()
            for half in (0, 1):
                other = gs[yy, pl.ds(2 * half, 2)].reshape(2 * PIECE, VW)
                gs[yy, pl.ds(2 * half, 2)] = (
                    (grad_half(c, yy, half) + f32(other)).astype(kind).reshape(2, PIECE, VW)
                )

        def first_sends(o):
            yy = (y + o) % 4
            for d in (2, 1, 3):
                outs[1, o, d] = send(
                    gs.at[yy, :, rows_of[1], lanes(turn("z", d))], r1.at[d - 1, yy],
                    peer("z", d), "rs1", 1, o, d,
                )
                outs[2, o, d] = send(
                    gs.at[yy, turn("x", d), rows_of[2], :], r2.at[d - 1, yy],
                    peer("x", d), "rs1", 2, o, d,
                )

        def first_sums(o):
            yy = (y + o) % 4
            for d in (1, 2, 3):
                outs[1, o, d].wait_recv()
            s1[yy] = add_up(gs[yy, :, rows_of[1], zc], [r1[d, yy] for d in range(3)]).astype(kind)
            if o:
                hop[1].append(send(s1.at[yy], q1.at[o - 1], peer("y", o), "rs2", 1, o))
            for d in (1, 2, 3):
                outs[2, o, d].wait_recv()
            s2[yy] = add_up(gs[yy, x, rows_of[2], :], [r2[d, yy] for d in range(3)]).astype(kind)
            for d in (2, 1, 3):
                hop[2].append(
                    send(
                        s2.at[yy, :, lanes(turn("z", d))], q2.at[d - 1, yy], peer("z", d),
                        "rs2", 2, o, d,
                    )
                )

        def pass_on(o):
            yy = (y + o) % 4
            side = 0 if o == 1 else 1
            relayed[side].wait_recv()
            for k in range(2):
                gs[yy, 2 * side + k, rows_of[0], :] = (
                    f32(gs[yy, 2 * side + k, rows_of[0], :]) + f32(rel[side, k])
                ).astype(kind)
            outs[0, o, 0] = send(
                gs.at[yy, :, rows_of[0], :], r0.at[side], peer("y", o), "rs1", 0, o
            )

        given, outs, hop = [], {}, {0: [], 1: [], 2: []}
        give(0, given)
        for i, o in enumerate(CHUNKS_OUT):
            if i + 1 < 4:
                give(i + 1, given)
            keep(i, given)
            if i == 0:
                relayed = [
                    send(
                        gs.at[turn("y", 2), pl.ds(2 * side, 2), rows_of[0], :], rel.at[side],
                        peer("y", 1 + 2 * side), "rs0", side,
                    )
                    for side in range(2)
                ]
            first_sends(o)
            if i >= 2:
                pass_on(CHUNKS_OUT[i - 1])
            if i:
                first_sums(CHUNKS_OUT[i - 1])
        first_sums(CHUNKS_OUT[3])
        for o in (1, 3):
            outs[0, o, 0].wait_recv()
        for d in (2, 1, 3, 0):
            xx = turn("x", d)
            s0[xx] = add_up(gs[y, xx, rows_of[0], :], [r0[0, xx], r0[1, xx]]).astype(kind)
            if d:
                hop[0].append(send(s0.at[xx], q0.at[d - 1], peer("x", d), "rs2", 0, d))
        sent += relayed + given[2:]
        sent += outs.values()
        last = {}
        for p in (1, 2, 0):
            for copy in hop[p]:
                copy.wait_recv()
            sent += hop[p]
            if p == 0:
                t0[...] = add_up(s0[x], [q0[d] for d in range(3)]).astype(kind)
                last[0] = [
                    send(t0.at[:, lanes(turn("z", d))], e0.at[d - 1], peer("z", d), "rs3", 0, d)
                    for d in (2, 1, 3)
                ]
            elif p == 1:
                t1[...] = add_up(s1[y], [q1[d] for d in range(3)]).astype(kind)
                last[1] = [
                    send(t1.at[turn("x", d)], e1.at[d - 1], peer("x", d), "rs3", 1, d)
                    for d in (2, 1, 3)
                ]
            else:
                t2[...] = add_up(s2[:, :, zc], [q2[d] for d in range(3)]).astype(kind)
                last[2] = [
                    send(t2.at[turn("y", d)], e2.at[d - 1], peer("y", d), "rs3", 2, d)
                    for d in (2, 1, 3)
                ]
        for p in (1, 2, 0):
            for copy in last[p]:
                copy.wait_recv()
            sent += last[p]
        gradient = jnp.concatenate(
            [
                add_up(t0[:, zc], [e0[d] for d in range(3)]),
                add_up(t1[x], [e1[d] for d in range(3)]),
                add_up(t2[y], [e2[d] for d in range(3)]),
            ],
            axis=0,
        )
        out_ref[u, own_rows, zc] = gradient.astype(jnp.bfloat16)
        if u == 0:
            for load in loads[6:]:
                load.wait()
            master, _, _ = adam_step(
                w_ref[own_rows, zc], m_ref[...], v_ref[...], gradient, PRIOR_STEPS + 1
            )
            wh[c, y, x, :, zc] = master.astype(jnp.bfloat16)
        else:
            shared += share(1)
            for copy in shared:
                copy.wait_recv()
            sent += shared
        for copy in sent:
            copy.wait_send()


def body(
    states, readout, logp_shift, advantage, response_mask, rollout_len, dest_slot,
    weight, moment1, moment2,
):
    row_index = jnp.arange(ROWS, dtype=jnp.int32)
    live = (row_index < rollout_len[0]) & (dest_slot >= 0)
    batch = jnp.where(live, (dest_slot % BAL) // MB, UPDATES)
    token = response_mask.astype(jnp.float32)
    lines = [logp_shift.astype(jnp.float32), advantage.astype(jnp.float32)]
    lines += [jnp.where(batch == k, token, 0.0) for k in range(UPDATES)]
    meta = jnp.pad(jnp.stack(lines), ((0, 4), (0, KPAD - ROWS)))
    bf16, full = jnp.bfloat16, jnp.float32
    vmem = pl.BlockSpec(memory_space=pltpu.VMEM)
    hbm = pl.BlockSpec(memory_space=pl.ANY)
    a, b, d = [size for _, size in PARTS]
    sums = [
        (2, 4, PIECE, VW), (4, 4, PIECE, VW), (2, 2, a, VW),
        (2, 4, a, VW), (3, 4, 4, b, LANES), (3, 4, d, VW),
        (4, a, VW), (4, 4, b, LANES), (4, d, VW),
        (3, a, VW), (3, 4, b, LANES), (3, 4, d, LANES),
        (a, VW), (4, b, LANES), (4, d, LANES),
        (3, a, LANES), (3, b, LANES), (3, d, LANES),
    ]
    gradients = pl.pallas_call(
        kernel,
        out_shape=jax.ShapeDtypeStruct((UPDATES,) + weight.shape, bf16),
        in_specs=[hbm, hbm, vmem, hbm, hbm, hbm],
        out_specs=vmem,
        scratch_shapes=[
            pltpu.VMEM((ROWS, D), bf16),
            pltpu.VMEM((D, KPAD), bf16),
            pltpu.VMEM((ROWS, VW), bf16),
            pltpu.VMEM((KPAD, 8), full),
            pltpu.VMEM((2 * PIECE, VW), full),
            pltpu.VMEM((PIECE, LANES), full),
            pltpu.VMEM((PIECE, LANES), full),
            pltpu.VMEM((2, 4, 4, PIECE, VW), bf16),
            pltpu.VMEM((ROWS, LANES), full),
            pltpu.VMEM((KPAD, VW), bf16),
            pltpu.VMEM((8, LANES), full),
            pltpu.VMEM((4, 3, 8, LANES), full),
            pltpu.SemaphoreType.DMA((8,)),
            pltpu.SemaphoreType.DMA((N_SEMS,)),
            pltpu.SemaphoreType.DMA((N_SEMS,)),
        ]
        + [pltpu.VMEM(dims, kind) for kind in SUM_TYPES for dims in sums],
        compiler_params=pltpu.CompilerParams(
            collective_id=0, has_side_effects=True, vmem_limit_bytes=58 * 1024 * 1024
        ),
    )(states, readout, meta, weight, moment1, moment2)
    master, one, two = weight, moment1, moment2
    for u in range(UPDATES):
        master, one, two = adam_step(
            master, one, two, gradients[u].astype(full), PRIOR_STEPS + u + 1
        )
    return master, one, two


def solution(mesh):
    rows = P(("dp", "shard"))
    return jax.shard_map(
        body,
        mesh=mesh,
        in_specs=(
            P(("dp", "shard"), None), P(("dp", "shard"), None), rows, rows, rows, rows, rows,
            P("shard", None), P("shard", None), P("shard", None),
        ),
        out_specs=(P("shard", None), P("shard", None), P("shard", None)),
        check_vma=False,
    )
```

time: 160 us -> 149 us (0.931)
  Pallas kernels: 149 us -> 141 us
  local copies, waits for them, and re-layouts: 8.25 us -> 1.4 us
  other arithmetic: 0.75 us -> 4.55 us
    pallas_call x1, Pallas kernels: 149 us -> 141 us  [body(): pl.pallas_call(kernel, out_shape=jax.ShapeDtypeStruct((UPDATES,) + weight...]
    unnamed x3 -> x6, local copies, waits for them, and re-layouts: 5.9 us -> 0.02 us
    sub x0 -> x1, other arithmetic: none -> 3.19 us  [adam_step(): master - LEARN_RATE * (first_hat / (jnp.sqrt(second_hat) + ADAM_EPS) + DE...]
where the time goes in v2:
time: 149 us; the launch traced here: 148 us
  Pallas kernels  141 us (95%)
  other arithmetic  4.55 us (3%)
  between operations  1.49 us (1%)
    pallas_call x1, Pallas kernels, body(): pl.pallas_call(kernel, out_shape=jax.ShapeDtypeStruct((UPDATES,) + weight...  141 us
    sub x1, other arithmetic, adam_step(): master - LEARN_RATE * (first_hat / (jnp.sqrt(second_hat) + ADAM_EPS) + DE...  3.19 us

profile of v2, /device:TPU:0, one launch (start us, length us, event | category | flops | bytes accessed | tf_op | source)
XLA Modules:
  0.0 148.4 jit_solution(9161246678560949446)
XLA Ops:
  0.6 0.0 copy-start.2
  0.6 0.0 copy-start.1
  0.7 0.0 copy-start
  1.4 0.7 reshape.10
  2.1 0.7 reshape.11
  2.8 0.7 convert_select_fusion.1
  3.6 0.6 select_maximum_fusion.meta_ref
  4.2 140.9 %shard_map.121 = bf16[2,320,512]{2,1,0:T(8,128)(2,1)} custom-call(bf16[864,5120]{1,0:T(8,128)(2,1)} %states_hbm.1, bf16[864,512]{1,0:T(8,128)(2,1)} %read_hbm.1, f32[8,896]{1,0:T(8,128)} %select_maximum_fusion.meta_ref, f32[320,512]{1,0:T(8,128)} %w_hbm.1, f32[320,512]{1,0:T(8,128)} %m_hbm.1, f32[320,512]{1,0:T(8,128)} %v_hbm.1), custom_call_target="tpu_custom_call" | custom-call | tf_op jit(solution)/shard_map/pallas_call | solution.py:518
  145.2 0.0 copy-done.2
  145.2 0.0 copy-done.1
  145.2 0.0 copy-done
  145.2 3.2 %multiply_subtract_fusion = (f32[320,512]{1,0:T(8,128)}, f32[320,512]{1,0:T(8,128)}, f32[320,512]{1,0:T(8,128)}) fusion(f32[320,512]{1,0:T(8,128)S(1)} %copy-done, f32[320,512]{1,0:T(8,128)S(1)} %copy-done.1, f32[320,512]{1,0:T(8,128)S(1)} %copy-done.2, bf16[2,320,512]{2,1,0:T(8,128)(2,1)} %shard_map.121), kind=kLoop, calls=%fused_computation.10 | loop fusion | flops 5242880 | bytes 4587520 | tf_op jit(solution)/shard_map/sub | solution.py:41
  (2 shorter events, 0.0 us)
Async XLA Ops:
  0.6 144.5 %copy-start.2 = (f32[320,512]{1,0:T(8,128)S(1)}, f32[320,512]{1,0:T(8,128)}, u32[]{:S(2)}) copy-start(f32[320,512]{1,0:T(8,128)} %v_hbm.1) | copy-start | bytes 1966084
  0.6 144.5 %copy-start.1 = (f32[320,512]{1,0:T(8,128)S(1)}, f32[320,512]{1,0:T(8,128)}, u32[]{:S(2)}) copy-start(f32[320,512]{1,0:T(8,128)} %m_hbm.1) | copy-start | bytes 1966084
  0.7 144.5 %copy-start = (f32[320,512]{1,0:T(8,128)S(1)}, f32[320,512]{1,0:T(8,128)}, u32[]{:S(2)}) copy-start(f32[320,512]{1,0:T(8,128)} %w_hbm.1) | copy-start | bytes 1966084

commit v3 on v2

v3 whole, which is shorter than its diff:
```python
import jax
import jax.numpy as jnp
from jax import lax
from jax.experimental import pallas as pl
from jax.experimental.pallas import tpu as pltpu
from jax.sharding import PartitionSpec as P

MESH = pl.DeviceIdType.MESH

BAL = 576
UPDATES = 2
PRIOR_STEPS = 100
MB = 288
ROWS = 864
KPAD = 896
D = 5120
VW = 512
PIECE = 160
LANES = 128
ROW_TILE = 288

BETA_ONE = 0.9
BETA_TWO = 0.999
LEARN_RATE = 0.001
DECAY_RATE = 0.01
ADAM_EPS = 1e-08
CLIP_EPS = 0.2

WHOLE = ((0, 64), (64, 48), (112, 48))
STREAMS = (
    (((0, 32), (32, 16), (48, 32)), ((80, 32), (112, 32), (144, 16))),
    (WHOLE,),
)
SUM_TYPES = (jnp.float32, jnp.bfloat16)
CHUNKS_IN = (0, 1, 3, 2)
CHUNKS_OUT = (2, 1, 3, 0)


def adam_step(master, moment_one, moment_two, gradient, step_num):
    moment_one = BETA_ONE * moment_one + (1.0 - BETA_ONE) * gradient
    moment_two = BETA_TWO * moment_two + (1.0 - BETA_TWO) * gradient * gradient
    first_hat = moment_one / (1.0 - BETA_ONE**step_num)
    second_hat = moment_two / (1.0 - BETA_TWO**step_num)
    master = master - LEARN_RATE * (
        first_hat / (jnp.sqrt(second_hat) + ADAM_EPS) + DECAY_RATE * master
    )
    return (master, moment_one, moment_two)


class Sems:
    def __init__(self, send, recv):
        self.send, self.recv, self.index = send, recv, {}

    def pair(self, *name):
        slot = self.index.setdefault(name, len(self.index))
        return self.send.at[slot], self.recv.at[slot]


N_SEMS = 400
N_SUMS = 13


def sums_of(parts):
    (_, a), (_, b), (_, d) = parts
    height = a + b + d
    return [
        (2, 4, height, VW), (4, 4, height, VW), (2, 2, a, VW),
        (2, 4, a, VW), (3, 4, 4, b, LANES), (3, 4, d, VW),
        (4, a, VW), (4, 4, b, LANES), (4, d, VW),
        (4, 4, a, LANES), (4, 4, b, LANES), (4, 4, d, LANES),
        (height, LANES),
    ]


def f32(value):
    return value.astype(jnp.float32)


def kernel(
    states_hbm, read_hbm, meta_ref, w_hbm, m_hbm, v_hbm, out_ref,
    st, st_t, rd, meta, w_ref, m_ref, v_ref, wh, acc, sc, cnt, cnt_in,
    load_sem, send_sem, recv_sem, *sums,
):
    dp, sh = lax.axis_index("dp"), lax.axis_index("shard")
    xl, z = dp // 4, dp % 4
    y, xh, c = sh // 4, (sh // 2) % 2, sh % 2
    x = xh * 2 + xl

    def device(x_, y_, z_, c_):
        return ((x_ % 2) * 4 + z_, y_ * 4 + (x_ // 2) * 2 + c_)

    def turn(axis, d):
        return ({"x": x, "y": y, "z": z}[axis] + d) % 4

    def peer(axis, d):
        to = turn(axis, d)
        return device(
            to if axis == "x" else x, to if axis == "y" else y, to if axis == "z" else z, c
        )

    twin = device(x, y, z, 1 - c)
    pair = xh * 2 + (1 - xl)
    replicas = [device(pair, y, turn("z", d), c) for d in range(4)]
    across_xy = [device(turn("x", 2), turn("y", d), z, c) for d in range(4)]
    flip = (x, pair, turn("x", 2), 3 - x)
    flipped = [device(to, y, z, c) for to in flip]

    def lanes(index):
        return pl.ds(pl.multiple_of(index * LANES, LANES), LANES)

    zc = lanes(z)
    sems = Sems(send_sem, recv_sem)

    def send(src, dst, to, *name):
        send_at, recv_at = sems.pair(*name)
        copy = pltpu.make_async_remote_copy(
            src_ref=src, dst_ref=dst, send_sem=send_at, recv_sem=recv_at,
            device_id=to, device_id_type=MESH,
        )
        copy.start()
        return copy

    own_rows = pl.ds(pl.multiple_of(xl * PIECE, PIECE), PIECE)

    loads = [pltpu.make_async_copy(w_hbm, w_ref, load_sem.at[0])]
    for k in range(4):
        cols = pl.ds(k * 1280, 1280)
        loads.append(
            pltpu.make_async_copy(states_hbm.at[:, cols], st.at[:, cols], load_sem.at[1 + k])
        )
    loads.append(pltpu.make_async_copy(read_hbm, rd, load_sem.at[5]))
    loads.append(pltpu.make_async_copy(m_hbm.at[own_rows, zc], m_ref, load_sem.at[6]))
    loads.append(pltpu.make_async_copy(v_hbm.at[own_rows, zc], v_ref, load_sem.at[7]))
    for load in loads:
        load.start()

    barrier = pltpu.get_barrier_semaphore()
    greeted = [twin]
    for e in range(4):
        for d in range(4):
            if d:
                greeted.append(device(turn("x", d), turn("y", e), z, c))
            if e:
                greeted.append(device(x, turn("y", e), turn("z", d), c))
            if e and d:
                greeted.append(device(turn("x", d), y, turn("z", e), c))
    for d in (1, 2, 3):
        greeted.append(device(x, y, turn("z", d), c))
    for to in greeted:
        pl.semaphore_signal(barrier, inc=1, device_id=to, device_id_type=MESH)

    for k in range(4):
        turned = meta_ref[pl.ds(8 * k, 8), :].T
        for j in range(KPAD // LANES):
            meta[pl.ds(j * LANES, LANES), k : k + 1] = turned[:, j : j + 1]
    lane = lax.broadcasted_iota(jnp.int32, (8, LANES), 1)
    cnt[...] = jnp.where(
        lane == 0,
        jnp.sum(jnp.sum(meta_ref[16:24, :], axis=0, keepdims=True), axis=1, keepdims=True),
        jnp.where(
            lane == 1,
            jnp.sum(jnp.sum(meta_ref[24:32, :], axis=0, keepdims=True), axis=1, keepdims=True),
            0.0,
        ),
    )
    sc[pl.ds(ROWS, KPAD - ROWS), :] = jnp.zeros((KPAD - ROWS, VW), jnp.bfloat16)
    loads[0].wait()
    for half in range(2):
        for (first, size), cols in zip(WHOLE, (slice(None), zc, slice(None))):
            rows = pl.ds(half * PIECE + first, size)
            wh[c, y, 2 * xh + half, pl.ds(first, size), cols] = w_ref[rows, cols].astype(
                jnp.bfloat16
            )
    pl.semaphore_wait(barrier, len(greeted))

    def count_start(stage, axis):
        return [
            send(cnt, cnt_in.at[stage, d - 1], peer(axis, d), "cnt", stage, d) for d in (1, 2, 3)
        ]

    def count_end(stage, copies):
        for copy in copies:
            copy.wait()
        total = cnt[...]
        for d in range(3):
            total = total + cnt_in[stage, d]
        cnt[...] = total

    def transpose_chunk(k):
        loads[1 + k].wait()

        def step(j, carry):
            cols = pl.ds(pl.multiple_of(k * 1280 + j * LANES, LANES), LANES)
            block = jnp.concatenate(
                [st[:, cols], jnp.zeros((KPAD - ROWS, LANES), jnp.bfloat16)], axis=0
            )
            st_t[cols, :] = block.T
            return carry

        lax.fori_loop(0, 10, step, 0)

    def fwd_chunk(yy, first):
        def step(i, carry):
            rows = pl.ds(pl.multiple_of(i * ROW_TILE, ROW_TILE), ROW_TILE)
            weight = jnp.concatenate(
                [
                    wh[core, yy, pl.ds(2 * half, 2)].reshape(2 * PIECE, VW)
                    for half in (0, 1)
                    for core in (0, 1)
                ],
                axis=0,
            )
            cols = pl.ds(pl.multiple_of(yy * 1280, 1280), 1280)
            proj = jnp.dot(st[rows, cols], weight, preferred_element_type=jnp.float32)
            prod = proj * f32(rd[rows, :])
            part = (
                prod[:, 0:128] + prod[:, 128:256] + prod[:, 256:384] + prod[:, 384:512]
            )
            if first:
                acc[rows, :] = part
            else:
                acc[rows, :] += part
            return carry

        lax.fori_loop(0, ROWS // ROW_TILE, step, 0)

    def scale_rows(u):
        total = jnp.maximum(cnt[0:1, u : u + 1], 1.0)

        def step(i, carry):
            rows = pl.ds(pl.multiple_of(i * ROW_TILE, ROW_TILE), ROW_TILE)
            shift, adv = meta[rows, 0:1], meta[rows, 1:2]
            weights = meta[rows, 2 + u : 3 + u]
            log_ratio = shift + jnp.sum(acc[rows, :], axis=1, keepdims=True)
            ratio = jnp.exp(log_ratio)
            clipped = jnp.clip(ratio, 1.0 - CLIP_EPS, 1.0 + CLIP_EPS)
            chosen = ratio * adv <= clipped * adv
            coeff = jnp.where(
                (weights > 0.0) & chosen, -(weights / total) * adv * ratio, 0.0
            )
            sc[rows, :] = (coeff * f32(rd[rows, :])).astype(jnp.bfloat16)
            return carry

        lax.fori_loop(0, ROWS // ROW_TILE, step, 0)

    def grad_block(core, yy, halves, first, height):
        blocks = []
        for half in halves:
            for low in (0, 1):
                start = yy * 1280 + half * 640 + core * 320 + low * PIECE + first
                blocks.append(st_t[pl.ds(pl.multiple_of(start, 16), height), :])
        product = jnp.dot(
            jnp.concatenate(blocks, axis=0), sc[...], preferred_element_type=jnp.float32
        )
        return product.reshape(len(blocks), height, VW)

    def add_up(own, parts):
        total = f32(own)
        for part in parts:
            total = total + f32(part)
        return total

    def share(u):
        block = out_ref.at[u, own_rows, zc]
        return [send(block, block, peer("z", d), "share", u, 0, d) for d in (1, 2, 3)] + [
            send(block, block, replicas[d], "share", u, 1, d) for d in range(4)
        ]

    class Gather:
        def __init__(self, name, parts):
            self.name = name
            self.rows = [pl.ds(first, size) for first, size in parts]
            self.sent, self.part_y, self.part_z, self.part_x = [], {}, {}, {}

        def ring(self, axis, block, *name, to=(1, 3, 2)):
            copies = {}
            for d in to:
                target = flipped[d] if axis == "x" else peer(axis, d)
                copies[d] = send(block, block, target, self.name, *name, d)
            self.sent.extend(copies.values())
            return copies

        def along_y(self, g):
            block = wh.at[c, y, flip[g], self.rows[0], :]
            self.part_y[g] = self.ring("y", block, "y", g, to=(1, 3))

        def along_z(self, o):
            block = wh.at[c, turn("y", o), :, self.rows[1], zc]
            self.part_z[o] = self.ring("z", block, "z", o)

        def along_x(self, o, to=(1, 3, 2)):
            block = wh.at[c, turn("y", o), x, self.rows[2], :]
            self.part_x[o] = self.ring("x", block, "x", o, to=to)

        def relay(self):
            self.relays = []
            for g, d in ((0, 1), (1, 3), (2, 1), (3, 3)):
                self.part_y[g][d].wait_recv()
                block = wh.at[c, turn("y", -d), flip[g], self.rows[0], :]
                self.relays.append(send(block, block, peer("y", d), self.name, "relay", g))
            self.sent += self.relays

        def arrived(self, o):
            if o == 2:
                for copy in self.relays:
                    copy.wait_recv()
            elif o:
                for g in range(4):
                    if (g, 4 - o) not in ((0, 1), (1, 3), (2, 1), (3, 3)):
                        self.part_y[g][4 - o].wait_recv()
            for copy in list(self.part_z[o].values()) + list(self.part_x[o].values()):
                copy.wait_recv()

    def gather_first(gather):
        second = gather.ring("x", wh.at[c, y, x, gather.rows[0], :], "ag2", 0, to=(3, 2))
        both = wh.at[c, y, pl.ds(2 * xh, 2), gather.rows[1], zc]
        plane = [send(both, both, across_xy[0], "ag2", 1, 0)]
        plane += [send(both, both, peer("y", d), "ag2", 1, 1, d) for d in (1, 2, 3)]
        plane += [send(both, both, across_xy[d], "ag2", 1, 2, d) for d in (1, 2, 3)]
        gather.sent += plane
        third = gather.ring("y", wh.at[c, y, x, gather.rows[2], :], "ag2", 2)
        gather.along_x(0, to=(3, 2))
        gather.along_y(0)
        gather.along_y(1)
        counting = count_start(0, "z")
        transpose_chunk(0)
        count_end(0, counting)
        counting = count_start(1, "x")
        for copy in plane:
            copy.wait_recv()
        gather.along_z(0)
        for g in (3, 2):
            second[g].wait_recv()
            gather.along_y(g)
        for o in (1, 3, 2):
            gather.along_z(o)
            third[4 - o].wait_recv()
            gather.along_x(o)
        transpose_chunk(1)
        count_end(1, counting)
        counting = count_start(2, "y")
        gather.relay()
        transpose_chunk(2)
        transpose_chunk(3)
        count_end(2, counting)
        return [send(cnt, cnt_in.at[3, 0], twin, "cnt", 3)]

    def gather_steps(gather):
        first = [
            gather.ring(axis, wh.at[c, y, x, gather.rows[p], zc], "ag1", p)
            for p, axis in enumerate("zxy")
        ]
        yield
        for copy in first[0].values():
            copy.wait_recv()
        second = [gather.ring("x", wh.at[c, y, x, gather.rows[0], :], "ag2", 0)]
        for copy in first[1].values():
            copy.wait_recv()
        second.append(gather.ring("y", wh.at[c, y, :, gather.rows[1], zc], "ag2", 1))
        for copy in first[2].values():
            copy.wait_recv()
        second.append(gather.ring("z", wh.at[c, :, x, gather.rows[2], zc], "ag2", 2))
        gather.along_y(0)
        gather.along_z(0)
        yield
        for g in (1, 3):
            second[0][g].wait_recv()
            gather.along_y(g)
        for copy in second[2].values():
            copy.wait_recv()
        gather.along_x(0)
        second[0][2].wait_recv()
        gather.along_y(2)
        for o in (1, 3, 2):
            second[1][4 - o].wait_recv()
            gather.along_z(o)
            gather.along_x(o)
        yield
        gather.relay()
        yield

    def reduce_steps(u, h, given, sent):
        kind, parts = SUM_TYPES[u], STREAMS[u][h]
        base, height = parts[0][0], sum(size for _, size in parts)
        rows = [pl.ds(first - base, size) for first, size in parts]
        at = N_SUMS * (h if u == 0 else len(STREAMS[0]))
        gsend, gs, rel, r0, r1, r2, s0, s1, s2, q0, q1, q2, total = sums[at : at + N_SUMS]
        groups = ((0, 1),) if height < PIECE else ((0,), (1,))
        outs, relayed, hop = {}, [], []

        def give(i):
            yy = turn("y", CHUNKS_OUT[i])
            if i >= 2:
                given[-2].wait_send()
            for halves in groups:
                gsend[i % 2, pl.ds(2 * halves[0], 2 * len(halves))] = grad_block(
                    1 - c, yy, halves, base, height
                ).astype(kind)
            given.append(send(gsend.at[i % 2], gs.at[yy], twin, "rsc", h, i))
            return given[-1]

        def keep(i):
            yy = turn("y", CHUNKS_OUT[i])
            gifts[i].wait_recv()
            for halves in groups:
                these = pl.ds(2 * halves[0], 2 * len(halves))
                gs[yy, these] = (
                    grad_block(c, yy, halves, base, height) + f32(gs[yy, these])
                ).astype(kind)

        def first_sends(o):
            yy = turn("y", o)
            for d in (2, 1, 3):
                outs[1, o, d] = send(
                    gs.at[yy, :, rows[1], lanes(turn("z", d))], r1.at[d - 1, yy],
                    peer("z", d), "rs1", h, 1, o, d,
                )
                outs[2, o, d] = send(
                    gs.at[yy, turn("x", d), rows[2], :], r2.at[d - 1, yy],
                    peer("x", d), "rs1", h, 2, o, d,
                )

        def first_sums(o):
            yy = turn("y", o)
            for d in (1, 2, 3):
                outs[1, o, d].wait_recv()
            s1[yy] = add_up(gs[yy, :, rows[1], zc], [r1[d, yy] for d in range(3)]).astype(kind)
            for d in (2, 1, 3, 0):
                if o or d:
                    xx = turn("x", d)
                    hop.append(
                        send(
                            s1.at[yy, xx], q1.at[o, d], device(xx, yy, z, c),
                            "rs2", h, 1, o, d,
                        )
                    )
            for d in (1, 2, 3):
                outs[2, o, d].wait_recv()
            s2[yy] = add_up(gs[yy, x, rows[2], :], [r2[d, yy] for d in range(3)]).astype(kind)
            for d in (2, 1, 3, 0):
                if o or d:
                    zz = turn("z", d)
                    hop.append(
                        send(
                            s2.at[yy, :, lanes(zz)], q2.at[o, d], device(x, yy, zz, c),
                            "rs2", h, 2, o, d,
                        )
                    )

        def pass_on(o):
            yy = turn("y", o)
            side = 0 if o == 1 else 1
            relayed[side].wait_recv()
            for k in range(2):
                gs[yy, 2 * side + k, rows[0], :] = (
                    f32(gs[yy, 2 * side + k, rows[0], :]) + f32(rel[side, k])
                ).astype(kind)
            outs[0, o, 0] = send(
                gs.at[yy, :, rows[0], :], r0.at[side], peer("y", o), "rs1", h, 0, o
            )

        gifts = [give(0)]
        for i, o in enumerate(CHUNKS_OUT):
            if i + 1 < 4:
                gifts.append(give(i + 1))
            keep(i)
            if i == 0:
                relayed += [
                    send(
                        gs.at[turn("y", 2), pl.ds(2 * side, 2), rows[0], :], rel.at[side],
                        peer("y", 1 + 2 * side), "rs0", h, side,
                    )
                    for side in range(2)
                ]
            first_sends(o)
            if i >= 2:
                pass_on(CHUNKS_OUT[i - 1])
            if i:
                first_sums(CHUNKS_OUT[i - 1])
            yield
        for o in (1, 3):
            outs[0, o, 0].wait_recv()
        for d in (2, 1, 3, 0):
            xx = turn("x", d)
            s0[xx] = add_up(gs[y, xx, rows[0], :], [r0[0, xx], r0[1, xx]]).astype(kind)
            for e in (2, 1, 3, 0):
                if d or e:
                    zz = turn("z", e)
                    hop.append(
                        send(
                            s0.at[xx, :, lanes(zz)], q0.at[d, e], device(xx, y, zz, c),
                            "rs2", h, 0, d, e,
                        )
                    )
        first_sums(CHUNKS_OUT[3])
        yield
        for copy in hop:
            copy.wait_recv()
        others = [(d, e) for d in range(4) for e in range(4) if d or e]
        owns = (s0[x, :, zc], s1[y, x], s2[y, :, zc])
        for p, got in enumerate((q0, q1, q2)):
            total[rows[p], :] = add_up(owns[p], [got[d, e] for d, e in others])
        gradient = total[...]
        out_ref[u, pl.ds(pl.multiple_of(xl * PIECE + base, 16), height), zc] = gradient.astype(
            jnp.bfloat16
        )
        if u == 0:
            if h == 0:
                for load in loads[6:]:
                    load.wait()
            these = pl.ds(base, height)
            master, _, _ = adam_step(
                w_ref[pl.ds(pl.multiple_of(xl * PIECE + base, 16), height), zc],
                m_ref[these, :], v_ref[these, :], gradient, PRIOR_STEPS + 1,
            )
            wh[c, y, x, these, zc] = master.astype(jnp.bfloat16)
        sent += relayed + gifts[2:] + list(outs.values()) + hop

    def stream_steps(h, gather, given, sent):
        yield from reduce_steps(0, h, given, sent)
        yield from gather_steps(gather)

    def multiply(u, gathers, shared):
        across = {}
        for i, o in enumerate(CHUNKS_IN):
            for a in CHUNKS_IN[:2] if i == 0 else CHUNKS_IN[i + 1 : i + 2]:
                for gather in gathers:
                    gather.arrived(a)
                block = wh.at[c, turn("y", a)]
                across[a] = send(block, block, twin, "agc", a)
                if u == 1 and a == CHUNKS_IN[3]:
                    shared += share(0)
            across[o].wait_recv()
            fwd_chunk(turn("y", o), i == 0)
        return list(across.values())

    shared = []
    gathers = [Gather("w0", WHOLE)]
    counting = gather_first(gathers[0])
    loads[5].wait()
    sent = multiply(0, gathers, shared)
    counting[0].wait()
    cnt[...] = cnt[...] + cnt_in[3, 0]
    scale_rows(0)
    for copy in sent + gathers[0].sent:
        copy.wait_send()

    sent, given = [], []
    gathers = [Gather("w1" + "ab"[h], parts) for h, parts in enumerate(STREAMS[0])]
    ahead, behind = [stream_steps(h, gathers[h], given, sent) for h in range(2)]
    for _ in range(4):
        next(ahead)
    running = [behind, ahead]
    while running:
        running = [steps for steps in running if next(steps, running) is not running]
    sent += multiply(1, gathers, shared)
    scale_rows(1)
    for copy in sent + gathers[0].sent + gathers[1].sent:
        copy.wait_send()

    sent = []
    for _ in reduce_steps(1, 0, [], sent):
        pass
    shared += share(1)
    for copy in shared:
        copy.wait_recv()
    for copy in sent + shared:
        copy.wait_send()


def body(
    states, readout, logp_shift, advantage, response_mask, rollout_len, dest_slot,
    weight, moment1, moment2,
):
    row_index = jnp.arange(ROWS, dtype=jnp.int32)
    live = (row_index < rollout_len[0]) & (dest_slot >= 0)
    batch = jnp.where(live, (dest_slot % BAL) // MB, UPDATES)
    token = response_mask.astype(jnp.float32)
    lines = [logp_shift.astype(jnp.float32), advantage.astype(jnp.float32)]
    lines += [jnp.where(batch == k, token, 0.0) for k in range(UPDATES)]
    meta = jnp.concatenate([jnp.pad(line, (0, 1024 - ROWS)) for line in lines])
    meta = meta.reshape(4 * 8, LANES)
    bf16, full = jnp.bfloat16, jnp.float32
    vmem = pl.BlockSpec(memory_space=pltpu.VMEM)
    hbm = pl.BlockSpec(memory_space=pl.ANY)
    sums = []
    for kind, streams in zip(SUM_TYPES, STREAMS):
        for parts in streams:
            *parcels, total = sums_of(parts)
            sums += [pltpu.VMEM(dims, kind) for dims in parcels] + [pltpu.VMEM(total, full)]
    gradients = pl.pallas_call(
        kernel,
        out_shape=jax.ShapeDtypeStruct((UPDATES,) + weight.shape, bf16),
        in_specs=[hbm, hbm, vmem, hbm, hbm, hbm],
        out_specs=vmem,
        scratch_shapes=[
            pltpu.VMEM((ROWS, D), bf16),
            pltpu.VMEM((D, KPAD), bf16),
            pltpu.VMEM((ROWS, VW), bf16),
            pltpu.VMEM((KPAD, 8), full),
            pltpu.VMEM((2 * PIECE, VW), full),
            pltpu.VMEM((PIECE, LANES), full),
            pltpu.VMEM((PIECE, LANES), full),
            pltpu.VMEM((2, 4, 4, PIECE, VW), bf16),
            pltpu.VMEM((ROWS, LANES), full),
            pltpu.VMEM((KPAD, VW), bf16),
            pltpu.VMEM((8, LANES), full),
            pltpu.VMEM((4, 3, 8, LANES), full),
            pltpu.SemaphoreType.DMA((8,)),
            pltpu.SemaphoreType.DMA((N_SEMS,)),
            pltpu.SemaphoreType.DMA((N_SEMS,)),
        ]
        + sums,
        compiler_params=pltpu.CompilerParams(
            collective_id=0, has_side_effects=True, vmem_limit_bytes=58 * 1024 * 1024
        ),
    )(states, readout, meta, weight, moment1, moment2)
    master, one, two = weight, moment1, moment2
    for u in range(UPDATES):
        master, one, two = adam_step(
            master, one, two, gradients[u].astype(full), PRIOR_STEPS + u + 1
        )
    return master, one, two


def solution(mesh):
    rows = P(("dp", "shard"))
    return jax.shard_map(
        body,
        mesh=mesh,
        in_specs=(
            P(("dp", "shard"), None), P(("dp", "shard"), None), rows, rows, rows, rows, rows,
            P("shard", None), P("shard", None), P("shard", None),
        ),
        out_specs=(P("shard", None), P("shard", None), P("shard", None)),
        check_vma=False,
    )
```

time: 149 us -> 155 us (1.040)
  Pallas kernels: 141 us -> 147 us
    pallas_call x1, Pallas kernels: 141 us -> 147 us  [body(): pl.pallas_call(kernel, out_shape=jax.ShapeDtypeStruct((UPDATES,) + weight...]
where the time goes in v3:
time: 155 us; the launch traced here: 154 us
  Pallas kernels  147 us (95%)
  other arithmetic  5.23 us (3%)
    pallas_call x1, Pallas kernels, body(): pl.pallas_call(kernel, out_shape=jax.ShapeDtypeStruct((UPDATES,) + weight...  147 us
    sub x1, other arithmetic, adam_step(): master - LEARN_RATE * (first_hat / (jnp.sqrt(second_hat) + ADAM_EPS) + DE...  3.19 us

profile of v3, /device:TPU:0, one launch (start us, length us, event | category | flops | bytes accessed | tf_op | source)
XLA Modules:
  0.0 153.9 jit_solution(17156374305828779399)
XLA Ops:
  0.6 0.0 copy-start.2
  0.6 0.0 copy-start.1
  0.7 0.0 copy-start
  1.4 0.7 convert_select_fusion.1
  2.2 0.7 bitcast_convert_fusion
  2.9 0.6 pad_maximum_fusion.meta_ref
  3.5 147.2 %shard_map.121 = bf16[2,320,512]{2,1,0:T(8,128)(2,1)} custom-call(bf16[864,5120]{1,0:T(8,128)(2,1)} %states_hbm.1, bf16[864,512]{1,0:T(8,128)(2,1)} %read_hbm.1, f32[32,128]{1,0:T(8,128)} %pad_maximum_fusion.meta_ref, f32[320,512]{1,0:T(8,128)} %w_hbm.1, f32[320,512]{1,0:T(8,128)} %m_hbm.1, f32[320,512]{1,0:T(8,128)} %v_hbm.1), custom_call_target="tpu_custom_call" | custom-call | tf_op jit(solution)/shard_map/pallas_call | solution.py:591
  150.7 0.0 copy-done.2
  150.7 0.0 copy-done.1
  150.7 0.0 copy-done
  150.7 3.2 %multiply_subtract_fusion = (f32[320,512]{1,0:T(8,128)}, f32[320,512]{1,0:T(8,128)}, f32[320,512]{1,0:T(8,128)}) fusion(f32[320,512]{1,0:T(8,128)S(1)} %copy-done, f32[320,512]{1,0:T(8,128)S(1)} %copy-done.1, f32[320,512]{1,0:T(8,128)S(1)} %copy-done.2, bf16[2,320,512]{2,1,0:T(8,128)(2,1)} %shard_map.121), kind=kLoop, calls=%fused_computation.10 | loop fusion | flops 5242880 | bytes 4587520 | tf_op jit(solution)/shard_map/sub | solution.py:44
  (1 shorter events, 0.0 us)
Async XLA Ops:
  0.6 150.0 %copy-start.2 = (f32[320,512]{1,0:T(8,128)S(1)}, f32[320,512]{1,0:T(8,128)}, u32[]{:S(2)}) copy-start(f32[320,512]{1,0:T(8,128)} %v_hbm.1) | copy-start | bytes 1966084
  0.6 150.0 %copy-start.1 = (f32[320,512]{1,0:T(8,128)S(1)}, f32[320,512]{1,0:T(8,128)}, u32[]{:S(2)}) copy-start(f32[320,512]{1,0:T(8,128)} %m_hbm.1) | copy-start | bytes 1966084
  0.7 150.0 %copy-start = (f32[320,512]{1,0:T(8,128)S(1)}, f32[320,512]{1,0:T(8,128)}, u32[]{:S(2)}) copy-start(f32[320,512]{1,0:T(8,128)} %w_hbm.1) | copy-start | bytes 1966084

commit v4 on v3

--- a/solution.py
+++ b/solution.py
@@ -28,7 +28,7 @@
 
 WHOLE = ((0, 64), (64, 48), (112, 48))
 STREAMS = (
-    (((0, 32), (32, 16), (48, 32)), ((80, 32), (112, 32), (144, 16))),
+    (WHOLE,),
     (WHOLE,),
 )
 SUM_TYPES = (jnp.float32, jnp.bfloat16)
@@ -57,6 +57,7 @@
 
 
 N_SEMS = 400
+RELAY_BY = (1, 3, 1, 3)
 N_SUMS = 13
 
 
@@ -77,7 +78,8 @@
 
 
 def kernel(
-    states_hbm, read_hbm, meta_ref, w_hbm, m_hbm, v_hbm, out_ref,
+    states_hbm, read_hbm, shift_ref, adv_ref, mask_ref, len_ref, slot_ref, w_hbm, m_hbm, v_hbm,
+    out_ref,
     st, st_t, rd, meta, w_ref, m_ref, v_ref, wh, acc, sc, cnt, cnt_in,
     load_sem, send_sem, recv_sem, *sums,
 ):
@@ -135,35 +137,11 @@
         load.start()
 
     barrier = pltpu.get_barrier_semaphore()
-    greeted = [twin]
-    for e in range(4):
-        for d in range(4):
-            if d:
-                greeted.append(device(turn("x", d), turn("y", e), z, c))
-            if e:
-                greeted.append(device(x, turn("y", e), turn("z", d), c))
-            if e and d:
-                greeted.append(device(turn("x", d), y, turn("z", e), c))
-    for d in (1, 2, 3):
-        greeted.append(device(x, y, turn("z", d), c))
+    greeted = [peer(axis, d) for axis in "xyz" for d in (1, 2, 3)] + [twin]
+    greeted += replicas[1:] + across_xy[1:]
     for to in greeted:
         pl.semaphore_signal(barrier, inc=1, device_id=to, device_id_type=MESH)
 
-    for k in range(4):
-        turned = meta_ref[pl.ds(8 * k, 8), :].T
-        for j in range(KPAD // LANES):
-            meta[pl.ds(j * LANES, LANES), k : k + 1] = turned[:, j : j + 1]
-    lane = lax.broadcasted_iota(jnp.int32, (8, LANES), 1)
-    cnt[...] = jnp.where(
-        lane == 0,
-        jnp.sum(jnp.sum(meta_ref[16:24, :], axis=0, keepdims=True), axis=1, keepdims=True),
-        jnp.where(
-            lane == 1,
-            jnp.sum(jnp.sum(meta_ref[24:32, :], axis=0, keepdims=True), axis=1, keepdims=True),
-            0.0,
-        ),
-    )
-    sc[pl.ds(ROWS, KPAD - ROWS), :] = jnp.zeros((KPAD - ROWS, VW), jnp.bfloat16)
     loads[0].wait()
     for half in range(2):
         for (first, size), cols in zip(WHOLE, (slice(None), zc, slice(None))):
@@ -172,6 +150,25 @@
                 jnp.bfloat16
             )
     pl.semaphore_wait(barrier, len(greeted))
+
+    def prepare():
+        def line(ref):
+            row = f32(ref[...]).reshape(1, ROWS)
+            return jnp.concatenate([row, jnp.zeros((1, KPAD - ROWS), jnp.float32)], axis=1)
+
+        slot = line(slot_ref)
+        place = lax.broadcasted_iota(jnp.int32, (1, KPAD), 1)
+        live = (place < len_ref[0]) & (slot >= 0.0) & (place < ROWS)
+        batch = jnp.floor((slot + 0.5) * (1.0 / MB))
+        odd = batch - 2.0 * jnp.floor(batch * 0.5)
+        token = jnp.where(live, line(mask_ref), 0.0)
+        tokens = [jnp.where(odd < 0.5, token, 0.0), jnp.where(odd < 0.5, 0.0, token)]
+        lines = [line(shift_ref), line(adv_ref)] + tokens
+        meta[...] = jnp.concatenate(lines + [jnp.zeros((4, KPAD), jnp.float32)], axis=0).T
+        lane = lax.broadcasted_iota(jnp.int32, (8, LANES), 1)
+        sums_now = [jnp.sum(row, axis=1, keepdims=True) for row in tokens]
+        cnt[...] = jnp.where(lane == 0, sums_now[0], jnp.where(lane == 1, sums_now[1], 0.0))
+        sc[pl.ds(ROWS, KPAD - ROWS), :] = jnp.zeros((KPAD - ROWS, VW), jnp.bfloat16)
 
     def count_start(stage, axis):
         return [
@@ -271,6 +268,7 @@
             self.name = name
             self.rows = [pl.ds(first, size) for first, size in parts]
             self.sent, self.part_y, self.part_z, self.part_x = [], {}, {}, {}
+            self.relays = []
 
         def ring(self, axis, block, *name, to=(1, 3, 2)):
             copies = {}
@@ -292,13 +290,12 @@
             block = wh.at[c, turn("y", o), x, self.rows[2], :]
             self.part_x[o] = self.ring("x", block, "x", o, to=to)
 
-        def relay(self):
-            self.relays = []
-            for g, d in ((0, 1), (1, 3), (2, 1), (3, 3)):
+        def relay(self, *blocks):
+            for g in blocks:
+                d = RELAY_BY[g]
                 self.part_y[g][d].wait_recv()
                 block = wh.at[c, turn("y", -d), flip[g], self.rows[0], :]
                 self.relays.append(send(block, block, peer("y", d), self.name, "relay", g))
-            self.sent += self.relays
 
         def arrived(self, o):
             if o == 2:
@@ -306,7 +303,7 @@
                     copy.wait_recv()
             elif o:
                 for g in range(4):
-                    if (g, 4 - o) not in ((0, 1), (1, 3), (2, 1), (3, 3)):
+                    if RELAY_BY[g] != 4 - o:
                         self.part_y[g][4 - o].wait_recv()
             for copy in list(self.part_z[o].values()) + list(self.part_x[o].values()):
                 copy.wait_recv()
@@ -322,6 +319,7 @@
         gather.along_x(0, to=(3, 2))
         gather.along_y(0)
         gather.along_y(1)
+        prepare()
         counting = count_start(0, "z")
         transpose_chunk(0)
         count_end(0, counting)
@@ -336,14 +334,19 @@
             gather.along_z(o)
             third[4 - o].wait_recv()
             gather.along_x(o)
-        transpose_chunk(1)
-        count_end(1, counting)
-        counting = count_start(2, "y")
-        gather.relay()
-        transpose_chunk(2)
-        transpose_chunk(3)
-        count_end(2, counting)
-        return [send(cnt, cnt_in.at[3, 0], twin, "cnt", 3)]
+
+        def between():
+            gather.relay(0, 1)
+            transpose_chunk(1)
+            count_end(1, counting)
+            counting_y = count_start(2, "y")
+            gather.relay(2, 3)
+            transpose_chunk(2)
+            transpose_chunk(3)
+            count_end(2, counting_y)
+            loads[5].wait()
+
+        return between
 
     def gather_steps(gather):
         first = [
@@ -376,8 +379,7 @@
             gather.along_z(o)
             gather.along_x(o)
         yield
-        gather.relay()
-        yield
+        gather.relay(0, 1)
 
     def reduce_steps(u, h, given, sent):
         kind, parts = SUM_TYPES[u], STREAMS[u][h]
@@ -473,11 +475,13 @@
                     for side in range(2)
                 ]
             first_sends(o)
-            if i >= 2:
-                pass_on(CHUNKS_OUT[i - 1])
-            if i:
-                first_sums(CHUNKS_OUT[i - 1])
+            if i == 2:
+                pass_on(CHUNKS_OUT[1])
+                pass_on(CHUNKS_OUT[2])
             yield
+        first_sums(CHUNKS_OUT[0])
+        first_sums(CHUNKS_OUT[1])
+        yield
         for o in (1, 3):
             outs[0, o, 0].wait_recv()
         for d in (2, 1, 3, 0):
@@ -492,6 +496,7 @@
                             "rs2", h, 0, d, e,
                         )
                     )
+        first_sums(CHUNKS_OUT[2])
         first_sums(CHUNKS_OUT[3])
         yield
         for copy in hop:
@@ -520,42 +525,53 @@
         yield from reduce_steps(0, h, given, sent)
         yield from gather_steps(gather)
 
-    def multiply(u, gathers, shared):
+    def multiply(gathers, between, before_last):
         across = {}
+
+        def cross(o):
+            for gather in gathers:
+                gather.arrived(o)
+            block = wh.at[c, turn("y", o)]
+            across[o] = send(block, block, twin, "agc", o)
+
+        cross(CHUNKS_IN[0])
+        between()
         for i, o in enumerate(CHUNKS_IN):
-            for a in CHUNKS_IN[:2] if i == 0 else CHUNKS_IN[i + 1 : i + 2]:
-                for gather in gathers:
-                    gather.arrived(a)
-                block = wh.at[c, turn("y", a)]
-                across[a] = send(block, block, twin, "agc", a)
-                if u == 1 and a == CHUNKS_IN[3]:
-                    shared += share(0)
+            if i < 3:
+                cross(CHUNKS_IN[i + 1])
+            if i == 2:
+                before_last()
             across[o].wait_recv()
             fwd_chunk(turn("y", o), i == 0)
-        return list(across.values())
-
-    shared = []
+        return list(across.values()) + [copy for gather in gathers for copy in gather.sent + gather.relays]
+
+    shared, counting = [], []
     gathers = [Gather("w0", WHOLE)]
-    counting = gather_first(gathers[0])
-    loads[5].wait()
-    sent = multiply(0, gathers, shared)
+    between = gather_first(gathers[0])
+    sent = multiply(
+        gathers, between, lambda: counting.append(send(cnt, cnt_in.at[3, 0], twin, "cnt", 3))
+    )
     counting[0].wait()
     cnt[...] = cnt[...] + cnt_in[3, 0]
     scale_rows(0)
-    for copy in sent + gathers[0].sent:
+    for copy in sent:
         copy.wait_send()
 
     sent, given = [], []
     gathers = [Gather("w1" + "ab"[h], parts) for h, parts in enumerate(STREAMS[0])]
-    ahead, behind = [stream_steps(h, gathers[h], given, sent) for h in range(2)]
+    running = [stream_steps(h, gathers[h], given, sent) for h in range(len(gathers))]
     for _ in range(4):
-        next(ahead)
-    running = [behind, ahead]
+        next(running[0])
+    running = running[::-1]
     while running:
         running = [steps for steps in running if next(steps, running) is not running]
-    sent += multiply(1, gathers, shared)
+    sent += multiply(
+        gathers,
+        lambda: [gather.relay(2, 3) for gather in gathers],
+        lambda: shared.extend(share(0)),
+    )
     scale_rows(1)
-    for copy in sent + gathers[0].sent + gathers[1].sent:
+    for copy in sent:
         copy.wait_send()
 
     sent = []
@@ -572,17 +588,10 @@
     states, readout, logp_shift, advantage, response_mask, rollout_len, dest_slot,
     weight, moment1, moment2,
 ):
-    row_index = jnp.arange(ROWS, dtype=jnp.int32)
-    live = (row_index < rollout_len[0]) & (dest_slot >= 0)
-    batch = jnp.where(live, (dest_slot % BAL) // MB, UPDATES)
-    token = response_mask.astype(jnp.float32)
-    lines = [logp_shift.astype(jnp.float32), advantage.astype(jnp.float32)]
-    lines += [jnp.where(batch == k, token, 0.0) for k in range(UPDATES)]
-    meta = jnp.concatenate([jnp.pad(line, (0, 1024 - ROWS)) for line in lines])
-    meta = meta.reshape(4 * 8, LANES)
     bf16, full = jnp.bfloat16, jnp.float32
     vmem = pl.BlockSpec(memory_space=pltpu.VMEM)
     hbm = pl.BlockSpec(memory_space=pl.ANY)
+    smem = pl.BlockSpec(memory_space=pltpu.SMEM)
     sums = []
     for kind, streams in zip(SUM_TYPES, STREAMS):
         for parts in streams:
@@ -591,7 +600,7 @@
     gradients = pl.pallas_call(
         kernel,
         out_shape=jax.ShapeDtypeStruct((UPDATES,) + weight.shape, bf16),
-        in_specs=[hbm, hbm, vmem, hbm, hbm, hbm],
+        in_specs=[hbm, hbm, vmem, vmem, vmem, smem, vmem, hbm, hbm, hbm],
         out_specs=vmem,
         scratch_shapes=[
             pltpu.VMEM((ROWS, D), bf16),
@@ -614,7 +623,10 @@
         compiler_params=pltpu.CompilerParams(
             collective_id=0, has_side_effects=True, vmem_limit_bytes=58 * 1024 * 1024
         ),
-    )(states, readout, meta, weight, moment1, moment2)
+    )(
+        states, readout, logp_shift, advantage, response_mask, rollout_len, dest_slot,
+        weight, moment1, moment2,
+    )
     master, one, two = weight, moment1, moment2
     for u in range(UPDATES):
         master, one, two = adam_step(

time: 155 us -> 142 us (0.916)
  Pallas kernels: 147 us -> 138 us
  other arithmetic: 5.23 us -> 3.19 us
    pallas_call x1, Pallas kernels: 147 us -> 138 us  [body(): pl.pallas_call(kernel, out_shape=jax.ShapeDtypeStruct((UPDATES,) + weight...]
where the time goes in v4:
time: 142 us
  Pallas kernels  138 us (97%)
  other arithmetic  3.19 us (2%)
  between operations  1.47 us (1%)
    pallas_call x1, Pallas kernels, body(): pl.pallas_call(kernel, out_shape=jax.ShapeDtypeStruct((UPDATES,) + weight...  138 us
    sub x1, other arithmetic, adam_step(): master - LEARN_RATE * (first_hat / (jnp.sqrt(second_hat) + ADAM_EPS) + DE...  3.19 us

profile of v4, /device:TPU:0, one launch (start us, length us, event | category | flops | bytes accessed | tf_op | source)
XLA Modules:
  0.0 142.3 jit_solution(17526817267886808215)
XLA Ops:
  0.6 0.0 copy-start.2
  0.6 0.0 copy-start.1
  0.7 0.0 copy-start
  1.4 137.6 %shard_map.121 = bf16[2,320,512]{2,1,0:T(8,128)(2,1)} custom-call(bf16[864,5120]{1,0:T(8,128)(2,1)} %states_hbm.1, bf16[864,512]{1,0:T(8,128)(2,1)} %read_hbm.1, bf16[864]{0:T(1024)(128)(2,1)} %shift_ref.1, bf16[864]{0:T(1024)(128)(2,1)} %adv_ref.1, s32[864]{0:T(1024)} %mask_ref.1, s32[1]{0:T(128)S(6)} %copy.13.len_ref, s32[864]{0:T(1024)} %slot_ref.1, ...), custom_call_target="tpu_custom_call" | custom-call | tf_op jit(solution)/shard_map/pallas_call | solution.py:600
  139.1 0.0 copy-done.2
  139.1 0.0 copy-done.1
  139.1 0.0 copy-done
  139.1 3.2 %multiply_subtract_fusion = (f32[320,512]{1,0:T(8,128)}, f32[320,512]{1,0:T(8,128)}, f32[320,512]{1,0:T(8,128)}) fusion(f32[320,512]{1,0:T(8,128)S(1)} %copy-done, f32[320,512]{1,0:T(8,128)S(1)} %copy-done.1, f32[320,512]{1,0:T(8,128)S(1)} %copy-done.2, bf16[2,320,512]{2,1,0:T(8,128)(2,1)} %shard_map.121), kind=kLoop, calls=%fused_computation.10 | loop fusion | flops 5242880 | bytes 4587520 | tf_op jit(solution)/shard_map/sub | solution.py:44
Async XLA Ops:
  0.6 138.4 %copy-start.2 = (f32[320,512]{1,0:T(8,128)S(1)}, f32[320,512]{1,0:T(8,128)}, u32[]{:S(2)}) copy-start(f32[320,512]{1,0:T(8,128)} %v_hbm.1) | copy-start | bytes 1966084
  0.6 138.4 %copy-start.1 = (f32[320,512]{1,0:T(8,128)S(1)}, f32[320,512]{1,0:T(8,128)}, u32[]{:S(2)}) copy-start(f32[320,512]{1,0:T(8,128)} %m_hbm.1) | copy-start | bytes 1966084
  0.7 138.4 %copy-start = (f32[320,512]{1,0:T(8,128)S(1)}, f32[320,512]{1,0:T(8,128)}, u32[]{:S(2)}) copy-start(f32[320,512]{1,0:T(8,128)} %w_hbm.1) | copy-start | bytes 1966084

commit v5 on v4

--- a/solution.py
+++ b/solution.py
@@ -39,8 +39,8 @@
 def adam_step(master, moment_one, moment_two, gradient, step_num):
     moment_one = BETA_ONE * moment_one + (1.0 - BETA_ONE) * gradient
     moment_two = BETA_TWO * moment_two + (1.0 - BETA_TWO) * gradient * gradient
-    first_hat = moment_one / (1.0 - BETA_ONE**step_num)
-    second_hat = moment_two / (1.0 - BETA_TWO**step_num)
+    first_hat = moment_one * (1.0 / (1.0 - BETA_ONE**step_num))
+    second_hat = moment_two * (1.0 / (1.0 - BETA_TWO**step_num))
     master = master - LEARN_RATE * (
         first_hat / (jnp.sqrt(second_hat) + ADAM_EPS) + DECAY_RATE * master
     )
@@ -58,17 +58,20 @@
 
 N_SEMS = 400
 RELAY_BY = (1, 3, 1, 3)
-N_SUMS = 13
-
-
-def sums_of(parts):
+N_SUMS = 19
+HOPS = (2, 2)
+
+
+def sums_of(parts, hops):
     (_, a), (_, b), (_, d) = parts
     height = a + b + d
     return [
         (2, 4, height, VW), (4, 4, height, VW), (2, 2, a, VW),
         (2, 4, a, VW), (3, 4, 4, b, LANES), (3, 4, d, VW),
         (4, a, VW), (4, 4, b, LANES), (4, d, VW),
-        (4, 4, a, LANES), (4, 4, b, LANES), (4, 4, d, LANES),
+        (4, a, VW) if hops == 2 else (4, 4, a, LANES), (4, 4, b, LANES), (4, 4, d, LANES),
+        (a, VW), (4, b, LANES), (4, d, LANES),
+        (4, a, LANES), (4, b, LANES), (4, d, LANES),
         (height, LANES),
     ]
 
@@ -138,7 +141,7 @@
 
     barrier = pltpu.get_barrier_semaphore()
     greeted = [peer(axis, d) for axis in "xyz" for d in (1, 2, 3)] + [twin]
-    greeted += replicas[1:] + across_xy[1:]
+    greeted += across_xy[1:]
     for to in greeted:
         pl.semaphore_signal(barrier, inc=1, device_id=to, device_id_type=MESH)
 
@@ -257,10 +260,11 @@
             total = total + f32(part)
         return total
 
-    def share(u):
-        block = out_ref.at[u, own_rows, zc]
-        return [send(block, block, peer("z", d), "share", u, 0, d) for d in (1, 2, 3)] + [
-            send(block, block, replicas[d], "share", u, 1, d) for d in range(4)
+    def share(u, p):
+        first, size = WHOLE[p]
+        block = out_ref.at[u, pl.ds(pl.multiple_of(xl * PIECE + first, 16), size), zc]
+        return [send(block, block, replicas[d], "share", u, p, 1, d) for d in range(4)] + [
+            send(block, block, peer("z", d), "share", u, p, 0, d) for d in (2, 1, 3)
         ]
 
     class Gather:
@@ -268,7 +272,7 @@
             self.name = name
             self.rows = [pl.ds(first, size) for first, size in parts]
             self.sent, self.part_y, self.part_z, self.part_x = [], {}, {}, {}
-            self.relays = []
+            self.relays, self.first = [], {}
 
         def ring(self, axis, block, *name, to=(1, 3, 2)):
             copies = {}
@@ -277,6 +281,10 @@
                 copies[d] = send(block, block, target, self.name, *name, d)
             self.sent.extend(copies.values())
             return copies
+
+        def begin(self, p):
+            block = wh.at[c, y, x, self.rows[p], zc]
+            self.first[p] = self.ring("zxy"[p], block, "ag1", p)
 
         def along_y(self, g):
             block = wh.at[c, y, flip[g], self.rows[0], :]
@@ -349,11 +357,7 @@
         return between
 
     def gather_steps(gather):
-        first = [
-            gather.ring(axis, wh.at[c, y, x, gather.rows[p], zc], "ag1", p)
-            for p, axis in enumerate("zxy")
-        ]
-        yield
+        first = gather.first
         for copy in first[0].values():
             copy.wait_recv()
         second = [gather.ring("x", wh.at[c, y, x, gather.rows[0], :], "ag2", 0)]
@@ -381,33 +385,37 @@
         yield
         gather.relay(0, 1)
 
-    def reduce_steps(u, h, given, sent):
+    def reduce_steps(u, h, given, sent, done):
         kind, parts = SUM_TYPES[u], STREAMS[u][h]
         base, height = parts[0][0], sum(size for _, size in parts)
         rows = [pl.ds(first - base, size) for first, size in parts]
         at = N_SUMS * (h if u == 0 else len(STREAMS[0]))
-        gsend, gs, rel, r0, r1, r2, s0, s1, s2, q0, q1, q2, total = sums[at : at + N_SUMS]
-        groups = ((0, 1),) if height < PIECE else ((0,), (1,))
-        outs, relayed, hop = {}, [], []
+        gsend, gs, rel, r0, r1, r2, s0, s1, s2, q0, q1, q2, *rest, total = sums[at : at + N_SUMS]
+        t0, t1, t2, e0, e1, e2 = rest
+        outs, relayed, hop = {}, [], {0: [], 1: [], 2: []}
 
         def give(i):
             yy = turn("y", CHUNKS_OUT[i])
             if i >= 2:
-                given[-2].wait_send()
-            for halves in groups:
-                gsend[i % 2, pl.ds(2 * halves[0], 2 * len(halves))] = grad_block(
-                    1 - c, yy, halves, base, height
-                ).astype(kind)
-            given.append(send(gsend.at[i % 2], gs.at[yy], twin, "rsc", h, i))
-            return given[-1]
+                for copy in given[-2]:
+                    copy.wait_send()
+            gift = []
+            for k in (0, 1):
+                these = pl.ds(2 * k, 2)
+                gsend[i % 2, these] = grad_block(1 - c, yy, (k,), base, height).astype(kind)
+                gift.append(
+                    send(gsend.at[i % 2, these], gs.at[yy, these], twin, "rsc", h, i, k)
+                )
+            given.append(gift)
+            return gift
 
         def keep(i):
             yy = turn("y", CHUNKS_OUT[i])
-            gifts[i].wait_recv()
-            for halves in groups:
-                these = pl.ds(2 * halves[0], 2 * len(halves))
+            for k in (0, 1):
+                these = pl.ds(2 * k, 2)
+                gifts[i][k].wait_recv()
                 gs[yy, these] = (
-                    grad_block(c, yy, halves, base, height) + f32(gs[yy, these])
+                    grad_block(c, yy, (k,), base, height) + f32(gs[yy, these])
                 ).astype(kind)
 
         def first_sends(o):
@@ -427,10 +435,12 @@
             for d in (1, 2, 3):
                 outs[1, o, d].wait_recv()
             s1[yy] = add_up(gs[yy, :, rows[1], zc], [r1[d, yy] for d in range(3)]).astype(kind)
+            if HOPS[u] == 2 and o:
+                hop[1].append(send(s1.at[yy], q1.at[o], peer("y", o), "rs2", h, 1, o))
             for d in (2, 1, 3, 0):
-                if o or d:
+                if HOPS[u] == 1 and (o or d):
                     xx = turn("x", d)
-                    hop.append(
+                    hop[1].append(
                         send(
                             s1.at[yy, xx], q1.at[o, d], device(xx, yy, z, c),
                             "rs2", h, 1, o, d,
@@ -440,9 +450,16 @@
                 outs[2, o, d].wait_recv()
             s2[yy] = add_up(gs[yy, x, rows[2], :], [r2[d, yy] for d in range(3)]).astype(kind)
             for d in (2, 1, 3, 0):
-                if o or d:
+                if HOPS[u] == 2 and d:
+                    hop[2].append(
+                        send(
+                            s2.at[yy, :, lanes(turn("z", d))], q2.at[d, yy], peer("z", d),
+                            "rs2", h, 2, o, d,
+                        )
+                    )
+                elif HOPS[u] == 1 and (o or d):
                     zz = turn("z", d)
-                    hop.append(
+                    hop[2].append(
                         send(
                             s2.at[yy, :, lanes(zz)], q2.at[o, d], device(x, yy, zz, c),
                             "rs2", h, 2, o, d,
@@ -487,10 +504,12 @@
         for d in (2, 1, 3, 0):
             xx = turn("x", d)
             s0[xx] = add_up(gs[y, xx, rows[0], :], [r0[0, xx], r0[1, xx]]).astype(kind)
+            if HOPS[u] == 2 and d:
+                hop[0].append(send(s0.at[xx], q0.at[d], peer("x", d), "rs2", h, 0, d))
             for e in (2, 1, 3, 0):
-                if d or e:
+                if HOPS[u] == 1 and (d or e):
                     zz = turn("z", e)
-                    hop.append(
+                    hop[0].append(
                         send(
                             s0.at[xx, :, lanes(zz)], q0.at[d, e], device(xx, y, zz, c),
                             "rs2", h, 0, d, e,
@@ -499,30 +518,59 @@
         first_sums(CHUNKS_OUT[2])
         first_sums(CHUNKS_OUT[3])
         yield
-        for copy in hop:
-            copy.wait_recv()
         others = [(d, e) for d in range(4) for e in range(4) if d or e]
-        owns = (s0[x, :, zc], s1[y, x], s2[y, :, zc])
-        for p, got in enumerate((q0, q1, q2)):
-            total[rows[p], :] = add_up(owns[p], [got[d, e] for d, e in others])
-        gradient = total[...]
-        out_ref[u, pl.ds(pl.multiple_of(xl * PIECE + base, 16), height), zc] = gradient.astype(
-            jnp.bfloat16
-        )
-        if u == 0:
-            if h == 0:
-                for load in loads[6:]:
-                    load.wait()
-            these = pl.ds(base, height)
-            master, _, _ = adam_step(
-                w_ref[pl.ds(pl.multiple_of(xl * PIECE + base, 16), height), zc],
-                m_ref[these, :], v_ref[these, :], gradient, PRIOR_STEPS + 1,
-            )
-            wh[c, y, x, these, zc] = master.astype(jnp.bfloat16)
-        sent += relayed + gifts[2:] + list(outs.values()) + hop
+        if u == 0 and h == 0:
+            for load in loads[6:]:
+                load.wait()
+        last = {}
+        if HOPS[u] == 2:
+            for p in (1, 2, 0):
+                for copy in hop[p]:
+                    copy.wait_recv()
+                if p == 0:
+                    t0[...] = add_up(s0[x], [q0[d] for d in (1, 2, 3)]).astype(kind)
+                elif p == 1:
+                    t1[...] = add_up(s1[y], [q1[d] for d in (1, 2, 3)]).astype(kind)
+                else:
+                    t2[...] = add_up(s2[:, :, zc], [q2[d] for d in (1, 2, 3)]).astype(kind)
+                last[p] = []
+                for d in (2, 1, 3):
+                    axis = "zxy"[p]
+                    block = (
+                        t0.at[:, lanes(turn("z", d))], t1.at[turn("x", d)], t2.at[turn("y", d)]
+                    )[p]
+                    last[p].append(
+                        send(block, (e0, e1, e2)[p].at[d], peer(axis, d), "rs3", h, p, d)
+                    )
+        for p in (1, 2, 0):
+            if HOPS[u] == 2:
+                for copy in last[p]:
+                    copy.wait_recv()
+                hop[p] += last[p]
+                own = (lambda: t0[:, zc], lambda: t1[x], lambda: t2[y])[p]()
+                got = [(e0, e1, e2)[p][d] for d in (1, 2, 3)]
+            else:
+                for copy in hop[p]:
+                    copy.wait_recv()
+                own = (lambda: s0[x, :, zc], lambda: s1[y, x], lambda: s2[y, :, zc])[p]()
+                got = [(q0, q1, q2)[p][d, e] for d, e in others]
+            total[rows[p], :] = add_up(own, got)
+            gradient = total[rows[p], :]
+            first, size = parts[p]
+            mine = pl.ds(pl.multiple_of(xl * PIECE + first, 16), size)
+            out_ref[u, mine, zc] = gradient.astype(jnp.bfloat16)
+            if u == 0:
+                these = pl.ds(first, size)
+                master, _, _ = adam_step(
+                    w_ref[mine, zc], m_ref[these, :], v_ref[these, :], gradient, PRIOR_STEPS + 1
+                )
+                wh[c, y, x, these, zc] = master.astype(jnp.bfloat16)
+            done(p)
+        sent += relayed + [copy for gift in gifts[2:] for copy in gift]
+        sent += list(outs.values()) + hop[0] + hop[1] + hop[2]
 
     def stream_steps(h, gather, given, sent):
-        yield from reduce_steps(0, h, given, sent)
+        yield from reduce_steps(0, h, given, sent, gather.begin)
         yield from gather_steps(gather)
 
     def multiply(gathers, between, before_last):
@@ -568,16 +616,15 @@
     sent += multiply(
         gathers,
         lambda: [gather.relay(2, 3) for gather in gathers],
-        lambda: shared.extend(share(0)),
+        lambda: shared.extend(copy for p in range(3) for copy in share(0, p)),
     )
     scale_rows(1)
     for copy in sent:
         copy.wait_send()
 
     sent = []
-    for _ in reduce_steps(1, 0, [], sent):
+    for _ in reduce_steps(1, 0, [], sent, lambda p: shared.extend(share(1, p))):
         pass
-    shared += share(1)
     for copy in shared:
         copy.wait_recv()
     for copy in sent + shared:
@@ -593,9 +640,9 @@
     hbm = pl.BlockSpec(memory_space=pl.ANY)
     smem = pl.BlockSpec(memory_space=pltpu.SMEM)
     sums = []
-    for kind, streams in zip(SUM_TYPES, STREAMS):
+    for kind, hops, streams in zip(SUM_TYPES, HOPS, STREAMS):
         for parts in streams:
-            *parcels, total = sums_of(parts)
+            *parcels, total = sums_of(parts, hops)
             sums += [pltpu.VMEM(dims, kind) for dims in parcels] + [pltpu.VMEM(total, full)]
     gradients = pl.pallas_call(
         kernel,

time: 142 us -> 139 us (0.979)
  Pallas kernels: 138 us -> 134 us
    pallas_call x1, Pallas kernels: 138 us -> 134 us  [body(): pl.pallas_call(kernel, out_shape=jax.ShapeDtypeStruct((UPDATES,) + weight...]
where the time goes in v5:
time: 139 us
  Pallas kernels  134 us (96%)
  other arithmetic  3.19 us (2%)
  between operations  1.47 us (1%)
    pallas_call x1, Pallas kernels, body(): pl.pallas_call(kernel, out_shape=jax.ShapeDtypeStruct((UPDATES,) + weight...  134 us
    sub x1, other arithmetic, adam_step(): master - LEARN_RATE * (first_hat / (jnp.sqrt(second_hat) + ADAM_EPS) + DE...  3.19 us

profile of v5, /device:TPU:0, one launch (start us, length us, event | category | flops | bytes accessed | tf_op | source)
XLA Modules:
  0.0 139.0 jit_solution(1198767621269411724)
XLA Ops:
  0.6 0.0 copy-start.2
  0.6 0.0 copy-start.1
  0.7 0.0 copy-start
  1.4 134.3 %shard_map.121 = bf16[2,320,512]{2,1,0:T(8,128)(2,1)} custom-call(bf16[864,5120]{1,0:T(8,128)(2,1)} %states_hbm.1, bf16[864,512]{1,0:T(8,128)(2,1)} %read_hbm.1, bf16[864]{0:T(1024)(128)(2,1)} %shift_ref.1, bf16[864]{0:T(1024)(128)(2,1)} %adv_ref.1, s32[864]{0:T(1024)} %mask_ref.1, s32[1]{0:T(128)S(6)} %copy.13.len_ref, s32[864]{0:T(1024)} %slot_ref.1, ...), custom_call_target="tpu_custom_call" | custom-call | tf_op jit(solution)/shard_map/pallas_call | solution.py:647
  135.8 0.0 copy-done.2
  135.8 0.0 copy-done.1
  135.8 0.0 copy-done
  135.8 3.2 %multiply_subtract_fusion = (f32[320,512]{1,0:T(8,128)}, f32[320,512]{1,0:T(8,128)}, f32[320,512]{1,0:T(8,128)}) fusion(f32[320,512]{1,0:T(8,128)S(1)} %copy-done, f32[320,512]{1,0:T(8,128)S(1)} %copy-done.1, f32[320,512]{1,0:T(8,128)S(1)} %copy-done.2, bf16[2,320,512]{2,1,0:T(8,128)(2,1)} %shard_map.121), kind=kLoop, calls=%fused_computation.10 | loop fusion | flops 5242880 | bytes 4587520 | tf_op jit(solution)/shard_map/sub | solution.py:44
Async XLA Ops:
  0.6 135.1 %copy-start.2 = (f32[320,512]{1,0:T(8,128)S(1)}, f32[320,512]{1,0:T(8,128)}, u32[]{:S(2)}) copy-start(f32[320,512]{1,0:T(8,128)} %v_hbm.1) | copy-start | bytes 1966084
  0.6 135.1 %copy-start.1 = (f32[320,512]{1,0:T(8,128)S(1)}, f32[320,512]{1,0:T(8,128)}, u32[]{:S(2)}) copy-start(f32[320,512]{1,0:T(8,128)} %m_hbm.1) | copy-start | bytes 1966084
  0.7 135.1 %copy-start = (f32[320,512]{1,0:T(8,128)S(1)}, f32[320,512]{1,0:T(8,128)}, u32[]{:S(2)}) copy-start(f32[320,512]{1,0:T(8,128)} %w_hbm.1) | copy-start | bytes 1966084

commit v6 on v5

--- a/solution.py
+++ b/solution.py
@@ -17,7 +17,7 @@
 VW = 512
 PIECE = 160
 LANES = 128
-ROW_TILE = 288
+ROW_TILE = 864
 
 BETA_ONE = 0.9
 BETA_TWO = 0.999

time: 139 us -> 136 us (0.978)
  Pallas kernels: 134 us -> 132 us
    pallas_call x1, Pallas kernels: 134 us -> 132 us  [body(): pl.pallas_call(kernel, out_shape=jax.ShapeDtypeStruct((UPDATES,) + weight...]
where the time goes in v6:
time: 136 us
  Pallas kernels  132 us (97%)
  other arithmetic  3.19 us (2%)
  between operations  1.47 us (1%)
    pallas_call x1, Pallas kernels, body(): pl.pallas_call(kernel, out_shape=jax.ShapeDtypeStruct((UPDATES,) + weight...  132 us
    sub x1, other arithmetic, adam_step(): master - LEARN_RATE * (first_hat / (jnp.sqrt(second_hat) + ADAM_EPS) + DE...  3.19 us

profile of v6, /device:TPU:0, one launch (start us, length us, event | category | flops | bytes accessed | tf_op | source)
XLA Modules:
  0.0 136.3 jit_solution(15041022141174252589)
XLA Ops:
  0.6 0.0 copy-start.2
  0.6 0.0 copy-start.1
  0.7 0.0 copy-start
  1.4 131.6 %shard_map.121 = bf16[2,320,512]{2,1,0:T(8,128)(2,1)} custom-call(bf16[864,5120]{1,0:T(8,128)(2,1)} %states_hbm.1, bf16[864,512]{1,0:T(8,128)(2,1)} %read_hbm.1, bf16[864]{0:T(1024)(128)(2,1)} %shift_ref.1, bf16[864]{0:T(1024)(128)(2,1)} %adv_ref.1, s32[864]{0:T(1024)} %mask_ref.1, s32[1]{0:T(128)S(6)} %copy.13.len_ref, s32[864]{0:T(1024)} %slot_ref.1, ...), custom_call_target="tpu_custom_call" | custom-call | tf_op jit(solution)/shard_map/pallas_call | solution.py:647
  133.1 0.0 copy-done.2
  133.1 0.0 copy-done.1
  133.1 0.0 copy-done
  133.1 3.2 %multiply_subtract_fusion = (f32[320,512]{1,0:T(8,128)}, f32[320,512]{1,0:T(8,128)}, f32[320,512]{1,0:T(8,128)}) fusion(f32[320,512]{1,0:T(8,128)S(1)} %copy-done, f32[320,512]{1,0:T(8,128)S(1)} %copy-done.1, f32[320,512]{1,0:T(8,128)S(1)} %copy-done.2, bf16[2,320,512]{2,1,0:T(8,128)(2,1)} %shard_map.121), kind=kLoop, calls=%fused_computation.10 | loop fusion | flops 5242880 | bytes 4587520 | tf_op jit(solution)/shard_map/sub | solution.py:44
Async XLA Ops:
  0.6 132.5 %copy-start.2 = (f32[320,512]{1,0:T(8,128)S(1)}, f32[320,512]{1,0:T(8,128)}, u32[]{:S(2)}) copy-start(f32[320,512]{1,0:T(8,128)} %v_hbm.1) | copy-start | bytes 1966084
  0.6 132.5 %copy-start.1 = (f32[320,512]{1,0:T(8,128)S(1)}, f32[320,512]{1,0:T(8,128)}, u32[]{:S(2)}) copy-start(f32[320,512]{1,0:T(8,128)} %m_hbm.1) | copy-start | bytes 1966084
  0.7 132.5 %copy-start = (f32[320,512]{1,0:T(8,128)S(1)}, f32[320,512]{1,0:T(8,128)}, u32[]{:S(2)}) copy-start(f32[320,512]{1,0:T(8,128)} %w_hbm.1) | copy-start | bytes 1966084
